TPU v7x, 128 devices: a whole 4x4x4 slice. The times are simulated.
128 devices in a mesh: wide: 8 (over y_hi, z), narrow: 16 (over x, y_lo, core).
Axes of the slice: x: 4, y: 4 (y_hi: 2, y_lo: 2; y = y_hi * 2 + y_lo), z: 4, core: 2. Of those that a mesh axis runs over, the one named last changes fastest.
Arguments:
- tokens: bfloat16 [256, 256, 768], P('wide', 'narrow'), may hold values from -6 to 6
- regions: int32 [256, 256], P('wide', 'narrow'), may hold values from 0 to 60
- w_qkv3: bfloat16 [768, 2304], replicated, may hold values from -0.21875 to 0.21875
- w_proj3: bfloat16 [768, 768], replicated, may hold values from -0.21875 to 0.21875
- bias_table3: float32 [24, 31, 31], replicated, may hold values from -3 to 3
- logit_scale3: float32 [24], replicated, may hold values from 2 to 20
- gain_attn3: float32 [768], replicated, may hold values from 0.1 to 1.9
- w_merge: bfloat16 [3072, 1536], replicated, may hold values from -0.109375 to 0.109375
- gain_merge: float32 [1536], replicated, may hold values from 0.1 to 1.9
- w_qkv4: bfloat16 [3, 1536, 1536], P(None, None, 'narrow'), may hold values from -0.15625 to 0.15625
- w_proj4: bfloat16 [1536, 1536], P('narrow'), may hold values from -0.15625 to 0.15625
- bias_table4: float32 [48, 31, 31], P('narrow'), may hold values from -3 to 3
- logit_scale4: float32 [48], P('narrow'), may hold values from 2 to 20
- gain_attn4: float32 [1536], replicated, may hold values from 0.1 to 1.9
- w_up4: bfloat16 [1536, 6144], P(None, 'narrow'), may hold values from -0.15625 to 0.15625
- w_down4: bfloat16 [6144, 1536], P('narrow'), may hold values from -0.078125 to 0.078125
- gain_mlp4: float32 [1536], replicated, may hold values from 0.1 to 1.9
Outputs:
- output: bfloat16 [128, 128, 1536], P('wide', 'narrow')
All inputs are finite; a program needn't handle non-finite values.
Results may differ from a plain program's by a relative error of at most 0.033.
Values may be sent and summed in bfloat16 or wider, within the bound.
A program may use at most 256 MiB of HBM per device.

v0:
```python
import jax
import jax.numpy as jnp
from jax import lax
from jax.sharding import PartitionSpec as P

HD = 32
WIN = 16
SHIFT = 8


def from_behind(block, axis, distance):
    devices = range(lax.axis_size(axis))
    route = [((i - distance) % len(devices), i) for i in devices]
    return lax.ppermute(block, axis, route)


def layer_norm(values, gain):
    center = jnp.mean(values, -1, keepdims=True)
    offset = values - center
    spread = jnp.mean(offset * offset, -1, keepdims=True)
    return offset * lax.rsqrt(spread + 1e-05) * gain


def window_bias(table, window):
    offsets = jnp.arange(window)
    relative = offsets[:, None] - offsets[None, :] + window - 1
    onehot = (relative[:, :, None] == jnp.arange(2 * window - 1)[None, None, :]).astype(jnp.float32)
    values = 16.0 * jax.nn.sigmoid(table)
    half_rows = jnp.einsum("hpq,acp->hacq", values, onehot, precision=lax.Precision.HIGHEST)
    full_bias = jnp.einsum("hacq,bdq->habcd", half_rows, onehot, precision=lax.Precision.HIGHEST)
    return full_bias.reshape(table.shape[0], window * window, window * window)


def to_windows(field, window):
    row_count, col_count = (field.shape[0], field.shape[1])
    trailing = field.shape[2:]
    blocked = field.reshape((row_count // window, window, col_count // window, window) + trailing)
    blocked = jnp.moveaxis(blocked, 2, 1)
    return blocked.reshape((-1, window * window) + trailing)


def from_windows(blocks, row_count, col_count, window):
    trailing = blocks.shape[2:]
    blocked = blocks.reshape((row_count // window, col_count // window, window, window) + trailing)
    blocked = jnp.moveaxis(blocked, 1, 2)
    return blocked.reshape((row_count, col_count) + trailing)


def attend(qkv_block, scale, bias, key_mask):
    query = qkv_block[:, :, 0].astype(jnp.float32)
    keys = qkv_block[:, :, 1].astype(jnp.float32)
    query = query / jnp.sqrt(jnp.sum(query * query, -1, keepdims=True) + 1e-06)
    keys = keys / jnp.sqrt(jnp.sum(keys * keys, -1, keepdims=True) + 1e-06)
    score = jnp.einsum("nqhd,nkhd->nhqk", query, keys, precision=lax.Precision.HIGHEST)
    score = score * scale[None, :, None, None] + bias[None]
    if key_mask is not None:
        score = score + key_mask[:, None]
    expo = jnp.exp(score)
    probs = (expo / jnp.sum(expo, -1, keepdims=True)).astype(jnp.bfloat16)
    context = jnp.einsum(
        "nhqk,nkhd->nqhd", probs, qkv_block[:, :, 2], preferred_element_type=jnp.float32
    )
    return context.astype(jnp.bfloat16)


def merge_pairs(field, w_merge, gain_merge):
    joined = jnp.concatenate(
        [field[0::2, 0::2], field[1::2, 0::2], field[0::2, 1::2], field[1::2, 1::2]], -1
    )
    row_count, col_count, depth = joined.shape
    merged_rows = jnp.dot(
        joined.reshape(row_count * col_count, depth), w_merge, preferred_element_type=jnp.float32
    )
    merged = layer_norm(merged_rows, gain_merge).astype(jnp.bfloat16)
    return merged.reshape(row_count, col_count, w_merge.shape[1])


def attention_terms(band_tokens, w_qkv, w_proj, table, scale):
    band_rows, band_cols, width4 = band_tokens.shape
    local_heads = scale.shape[0]
    qkv_four = jnp.einsum(
        "rcf,jfo->rcjo", band_tokens, w_qkv, preferred_element_type=jnp.float32
    ).astype(jnp.bfloat16)
    four_wins = to_windows(qkv_four.reshape(band_rows, band_cols, 3, local_heads, HD), WIN)
    context4 = attend(four_wins, scale, window_bias(table, WIN), None)
    context4 = from_windows(context4, band_rows, band_cols, WIN).reshape(-1, local_heads * HD)
    return jnp.dot(context4, w_proj, preferred_element_type=jnp.float32).reshape(
        band_rows, band_cols, width4
    )


def mlp_terms(hidden, w_up, w_down):
    band_rows, band_cols, width4 = hidden.shape
    inner_act = jax.nn.gelu(
        jnp.dot(hidden.reshape(-1, width4), w_up, preferred_element_type=jnp.float32),
        approximate=False,
    ).astype(jnp.bfloat16)
    return jnp.dot(inner_act, w_down, preferred_element_type=jnp.float32).reshape(
        band_rows, band_cols, width4
    )


def per_device(
    tokens,
    regions,
    w_qkv3,
    w_proj3,
    bias_table3,
    logit_scale3,
    gain_attn3,
    w_merge,
    gain_merge,
    w_qkv4,
    w_proj4,
    bias_table4,
    logit_scale4,
    gain_attn4,
    w_up4,
    w_down4,
    gain_mlp4,
):
    tile_rows, tile_cols, width3 = tokens.shape
    heads3 = width3 // HD
    top_rows = from_behind(tokens[:SHIFT], "wide", -1)
    lifted = jnp.concatenate([tokens[SHIFT:], top_rows], 0)
    left_cols = from_behind(lifted[:, :SHIFT], "narrow", -1)
    rolled = jnp.concatenate([lifted[:, SHIFT:], left_cols], 1)
    qkv_rows = jnp.dot(
        rolled.reshape(-1, width3), w_qkv3, preferred_element_type=jnp.float32
    ).astype(jnp.bfloat16)
    qkv_wins = to_windows(qkv_rows.reshape(tile_rows, tile_cols, 3, heads3, HD), WIN)
    window_labels = to_windows(regions, WIN)
    key_mask = jnp.where(
        window_labels[:, :, None] == window_labels[:, None, :], 0.0, -100.0
    ).astype(jnp.float32)
    context = attend(qkv_wins, logit_scale3, window_bias(bias_table3, WIN), key_mask)
    context = from_windows(context, tile_rows, tile_cols, WIN).reshape(-1, width3)
    projected = jnp.dot(context, w_proj3, preferred_element_type=jnp.float32)
    shifted_out = (
        rolled.reshape(-1, width3).astype(jnp.float32) + layer_norm(projected, gain_attn3)
    ).astype(jnp.bfloat16)
    shifted_out = shifted_out.reshape(tile_rows, tile_cols, width3)
    lower_rows = from_behind(shifted_out[tile_rows - SHIFT :], "wide", 1)
    lowered = jnp.concatenate([lower_rows, shifted_out[: tile_rows - SHIFT]], 0)
    side_cols = from_behind(lowered[:, tile_cols - SHIFT :], "narrow", 1)
    merged = merge_pairs(
        jnp.concatenate([side_cols, lowered[:, : tile_cols - SHIFT]], 1), w_merge, gain_merge
    )
    band_tokens = lax.all_gather(merged, "narrow", axis=1, tiled=True)
    band_rows, band_cols, width4 = band_tokens.shape
    partial_value = attention_terms(band_tokens, w_qkv4, w_proj4, bias_table4, logit_scale4)
    share_cols = band_cols // lax.axis_size("narrow")
    col_start = lax.axis_index("narrow") * share_cols
    total_sum = lax.psum(partial_value.astype(jnp.bfloat16), "narrow").astype(jnp.float32)
    hidden = (band_tokens.astype(jnp.float32) + layer_norm(total_sum, gain_attn4)).astype(
        jnp.bfloat16
    )
    hidden_own = lax.dynamic_slice_in_dim(hidden, col_start, share_cols, 1)
    down_terms = mlp_terms(hidden, w_up4, w_down4)
    own_terms = lax.psum_scatter(
        down_terms.astype(jnp.bfloat16), "narrow", scatter_dimension=1, tiled=True
    ).astype(jnp.float32)
    return (hidden_own.astype(jnp.float32) + layer_norm(own_terms, gain_mlp4)).astype(jnp.bfloat16)


def solution(mesh):
    placed = (
        P("wide", "narrow", None),
        P("wide", "narrow"),
        P(),
        P(),
        P(),
        P(),
        P(),
        P(),
        P(),
        P(None, None, "narrow"),
        P("narrow", None),
        P("narrow", None, None),
        P("narrow"),
        P(),
        P(None, "narrow"),
        P("narrow", None),
        P(),
    )
    return jax.shard_map(
        per_device, mesh=mesh, in_specs=placed, out_specs=P("wide", "narrow", None), check_vma=False
    )
```

profile of v0, /device:TPU:1, one launch (start us, length us, event | category | flops | bytes accessed | tf_op | source)
XLA Modules:
  0.0 555.4 jit_solution(6683015345354005938)
XLA Ops:
  7.6 7.3 %collective-permute-start = (bf16[8,16,768]{2,1,0:T(8,128)(2,1)S(1)}, bf16[8,16,768]{2,1,0:T(8,128)(2,1)S(1)}, u32[]{:S(2)}, u32[]{:S(2)}) collective-permute-start(bf16[8,16,768]{2,1,0:T(8,128)(2,1)S(1)} %slice.61), channel_id=1, source_target_pairs={{16,0},{32,16},{48,32},{64,48},{80,64},{96,80},{112,96},{0,112},{1... | collective-permute-start | bytes 589832 | tf_op jit(solution)/shard_map/ppermute | solution.py:14
  19.4 2.0 collective-permute-start.1
  21.5 17.1 %convolution_bitcast_fusion = f32[24,16,16,16,16]{0,4,3,1,2:T(8,128)} fusion(f32[24,16,16,31]{3,2,0,1:T(8,128)S(1)} %convolution_bitcast_fusion.2, s32[16,16]{1,0:T(8,128)S(1)} %subtract_add_fusion), kind=kOutput, calls=%fused_computation.4 | convolution fusion | flops 585113344 | bytes 7054336 | tf_op jit(solution)/shard_map/hacq,bdq->habcd/dot_general | solution.py:30
  40.0 51.0 %copy.76 = f32[24,16,16,16,16]{2,1,4,3,0:T(8,128)} copy(f32[24,16,16,16,16]{0,4,3,1,2:T(8,128)} %convolution_bitcast_fusion) | data formatting | bytes 12582912 | tf_op jit(solution)/shard_map/add | solution.py:55
  91.0 34.6 %reshape.153 = f32[24,256,256]{1,2,0:T(8,128)} reshape(f32[24,16,16,16,16]{2,1,4,3,0:T(8,128)} %copy.76) | data formatting | bytes 12582912 | tf_op jit(solution)/shard_map/add | solution.py:55
  128.6 3.4 convolution_convert_fusion.2
  132.1 4.3 copy.45
  136.3 5.0 reshape_transpose_reshape_reshape.3
  144.7 17.0 %fusion.6 = (f32[2,24,256]{2,1,0:T(8,128)S(1)}, f32[2,24,256,256]{2,3,1,0:T(8,128)}) fusion(f32[2,256,256]{1,2,0:T(8,128)S(1)} %copy-done.6, f32[24,256,256]{1,2,0:T(8,128)} %reshape.153, f32[24]{0:T(128)S(1)} %copy-done.14, f32[2,256,24,32]{1,0,3,2:T(2,128)S(1)} %get-tuple-element.10, f32[2,256,24,32]{1,0,3,2:T(2,128)S(1)} %get-tuple-element.9), kind=kOutput, calls=%fused_computation.11 | convolution fusion | flops 1220530176 | bytes 22593632 | tf_op jit(solution)/shard_map/nqhd,nkhd->nhqk/dot_general | solution.py:54
  161.8 6.5 %fusion.69 = bf16[2,256,24,32]{1,3,2,0:T(8,128)(2,1)S(1)} fusion(f32[2,24,256,256]{2,3,1,0:T(8,128)} %get-tuple-element.14, f32[2,24,256]{2,1,0:T(8,128)S(1)} %get-tuple-element.13, f32[2,256,256]{1,2,0:T(8,128)S(1)} %copy-done.6, f32[24,256,256]{1,2,0:T(8,128)S(1)} %bitcast.156, f32[24]{0:T(128)S(1)} %copy-done.14, ...), kind=kOutput, calls=%fused_computation.100 | convolution fusion | flops 217448448 | bytes 21020768 | tf_op jit(solution)/shard_map/nhqk,nkhd->nqhd/dot_general | solution.py:60
  171.3 8.8 %collective-permute-done.2 = bf16[8,16,768]{2,1,0:T(8,128)(2,1)S(1)} collective-permute-done((bf16[8,16,768]{2,1,0:T(8,128)(2,1)S(1)}, bf16[8,16,768]{2,1,0:T(8,128)(2,1)S(1)}, u32[]{:S(2)}, u32[]{:S(2)}) %collective-permute-start.2) | collective-permute-done | bytes 196640 | tf_op jit(solution)/shard_map/ppermute | solution.py:14
  180.2 3.1 collective-permute-start.3
  183.3 4.7 collective-permute-done.3
  190.6 5.2 fusion.146
  197.4 4.9 convolution_bitcast_fusion.1
  202.3 8.9 %copy.77 = f32[3,16,16,16,16]{2,1,4,3,0:T(8,128)} copy(f32[3,16,16,16,16]{3,4,1,0,2:T(8,128)} %convolution_bitcast_fusion.1) | data formatting | bytes 1572864 | tf_op jit(solution)/shard_map/add | solution.py:55
  211.1 5.1 reshape.154
  216.2 23.5 %all-gather.2.cloned.1.call-done = bf16[16,128,1536]{2,1,0:T(8,128)(2,1)} async-done(((bf16[16,8,1536]{2,1,0:T(8,128)(2,1)}), bf16[16,128,1536]{2,1,0:T(8,128)(2,1)}) %all-gather.2.cloned.1.call-update) | async-done | bytes 6291472 | tf_op jit(solution)/shard_map/all_gather | solution.py:149
  239.7 4.8 fusion.65
  245.4 6.3 %reshape_reshape.4 = bf16[1,16,8,16,3,3,32]{6,5,3,2,4,1,0:T(4,128)(2,1)} reshape(bf16[16,128,3,96]{3,1,2,0:T(8,128)(2,1)S(1)} %copy.56) | data formatting | bytes 2359296 | tf_op jit(solution)/shard_map/reshape;reshape | solution.py:37
  251.7 4.0 copy.57
  257.6 7.3 %fusion.10 = (f32[8,3,256]{2,1,0:T(4,128)S(1)}, f32[8,3,256,256]{2,3,1,0:T(8,128)S(1)}) fusion(f32[3,256,256]{1,2,0:T(8,128)S(1)} %reshape.154, f32[3]{0:T(128)S(1)} %copy-done.19, f32[8,256,3]{1,2,0:T(4,128)S(1)} %add_sqrt_fusion.2, bf16[8,256,3,3,32]{4,1,3,2,0:T(8,128)(2,1)S(1)} %bitcast.160, f32[8,256,3]{1,2,0:T(4,128)S(1)} %add_sqrt_fusion.3), kind=kOutput, calls=%fused_computation.19 | convolution fusion | flops 609478656 | bytes 10314240 | tf_op jit(solution)/shard_map/nqhd,nkhd->nhqk/dot_general | solution.py:54
  266.4 1.9 copy.64
  268.3 3.6 copy.65
  272.9 4.4 convolution_convert_fusion.1
  277.4 154.2 %all-reduce.2.cloned.1.call-done = bf16[16,128,1536]{2,1,0:T(8,128)(2,1)} async-done(((bf16[16,128,1536]{2,1,0:T(8,128)(2,1)}), bf16[16,128,1536]{2,1,0:T(8,128)(2,1)}) %all-reduce.2.cloned.1.call-update) | async-done | bytes 6291472 | tf_op jit(solution)/shard_map/psum | solution.py:154
  431.5 3.8 convert_reduce_fusion
  438.0 7.7 %fusion.5 = bf16[16,128,1536]{2,1,0:T(8,128)(2,1)} fusion(bf16[16,128,1536]{2,1,0:T(8,128)(2,1)S(1)} %copy-done.2, bf16[16,128,1536]{2,1,0:T(8,128)(2,1)} %all-gather.2.cloned.1.call-done, f32[1536]{0:T(1024)S(1)} %copy-done.9, f32[16,128]{1,0:T(8,128)S(1)} %add_rsqrt_fusion.1, f32[16,128]{1,0:T(8,128)S(1)} %broadcast_multiply_fusion.1), kind=kLoop, calls=%fused_computation.8 | loop fusion | flops 22020096 | bytes 18896896 | tf_op jit(solution)/shard_map/convert_element_type | solution.py:155
  445.7 16.4 %convolution_convert_fusion = bf16[2048,1536]{1,0:T(8,128)(2,1)} fusion(bf16[384,1536]{1,0:T(8,128)(2,1)S(1)} %copy-done.16, bf16[2048,1536]{1,0:T(8,128)(2,1)} %bitcast.162, bf16[1536,384]{1,0:T(8,128)(2,1)S(1)} %copy-done.17), kind=kOutput, calls=%fused_computation.12 | convolution fusion | flops 4886102016 | bytes 14942208 | tf_op jit(solution)/shard_map/dot_general | solution.py:98
  462.1 6.1 %copy.85 = bf16[16,8,16,1536]{3,1,2,0:T(8,128)(2,1)} copy(bf16[16,8,16,1536]{3,1,0,2:T(8,128)(2,1)} %bitcast.163) | data formatting | bytes 12582912
  468.2 76.7 %reduce-scatter.4.cloned.1.call-done = bf16[8,24576]{1,0:T(8,128)(2,1)} async-done(((bf16[128,24576]{1,0:T(8,128)(2,1)}), bf16[8,24576]{1,0:T(8,128)(2,1)}) %reduce-scatter.4.cloned.1.call-update) | async-done | bytes 393232
  546.6 2.1 fusion.78
  (104 shorter events, 30.1 us)
Async XLA Ops:
  6.5 122.1 %copy-start = (bf16[768,2304]{1,0:T(8,128)(2,1)S(1)}, bf16[768,2304]{1,0:T(8,128)(2,1)}, u32[]{:S(2)}) copy-start(bf16[768,2304]{1,0:T(8,128)(2,1)} %param.19) | copy-start | bytes 10616836
  6.5 233.2 %all-gather.2.cloned.1.call-start = ((), (), s32[]{:S(2)}) async-start(), calls=%async_computation.1 | async-start | bytes 6684672 | tf_op jit(solution)/shard_map/all_gather | solution.py:149
  6.5 12.0 %slice-start.3 = ((bf16[32,16,768]{2,1,0:T(8,128)(2,1)}), bf16[24,16,768]{2,1,0:T(8,128)(2,1)S(1)}, s32[]{:S(2)}) async-start(bf16[32,16,768]{2,1,0:T(8,128)(2,1)} %param.17), calls=%async_computation.7 | async-start | bytes 1179648 | tf_op jit(solution)/shard_map/slice | solution.py:125
  7.6 10.9 %collective-permute-start = (bf16[8,16,768]{2,1,0:T(8,128)(2,1)S(1)}, bf16[8,16,768]{2,1,0:T(8,128)(2,1)S(1)}, u32[]{:S(2)}, u32[]{:S(2)}) collective-permute-start(bf16[8,16,768]{2,1,0:T(8,128)(2,1)S(1)} %slice.61), channel_id=1, source_target_pairs={{16,0},{32,16},{48,32},{64,48},{80,64},{96,80},{112,96},{0,112},{1... | collective-permute-start | bytes 589832 | tf_op jit(solution)/shard_map/ppermute | solution.py:14
  19.4 19.1 %copy-start.12 = (s32[32,16]{0,1:T(8,128)S(1)}, s32[32,16]{0,1:T(8,128)}, u32[]{:S(2)}) copy-start(s32[32,16]{0,1:T(8,128)} %param.18) | copy-start | bytes 6148
  19.4 107.1 %collective-permute-start.1 = (bf16[32,8,768]{2,1,0:T(8,128)(2,1)}, bf16[32,8,768]{2,1,0:T(8,128)(2,1)}, u32[]{:S(2)}, u32[]{:S(2)}) collective-permute-start(bf16[32,8,768]{2,1,0:T(8,128)(2,1)} %get-tuple-element.12), channel_id=1, source_target_pairs={{1,0},{2,1},{3,2},{4,3},{5,4},{6,5},{7,6},{8,7},{9,8},{10,9},{11,1... | collective-permute-start | bytes 1179656 | tf_op jit(solution)/shard_map/ppermute | solution.py:14
  127.7 0.9 copy-start.4
  141.3 3.3 copy-start.3
  143.1 1.6 copy-start.6
  143.1 1.6 copy-start.14
  143.2 18.5 %slice-start = ((s8[6291456]{0:T(1024)(128)(4,1)}), s8[4194304]{0:T(1024)(128)(4,1)S(1)}, s32[]{:S(2)}) async-start(s8[6291456]{0:T(1024)(128)(4,1)} %bitcast.155), calls=%async_computation.4 | async-start | bytes 8388608
  144.7 17.1 %slice-start.1 = ((s8[6291456]{0:T(1024)(128)(4,1)}), s8[2097152]{0:T(1024)(128)(4,1)S(1)}, s32[]{:S(2)}) async-start(s8[6291456]{0:T(1024)(128)(4,1)} %bitcast.155), calls=%async_computation.5 | async-start | bytes 4194304
  144.7 17.1 %slice-start.2 = ((bf16[2,256,3,24,32]{1,0,4,3,2:T(2,128)(2,1)}), bf16[2,256,1,24,32]{1,0,4,3,2:T(2,128)(2,1)S(1)}, s32[]{:S(2)}) async-start(bf16[2,256,3,24,32]{1,0,4,3,2:T(2,128)(2,1)} %copy-done.3), calls=%async_computation.6 | async-start | bytes 1572864 | tf_op jit(solution)/shard_map/slice | solution.py:61
  168.3 1.3 copy-start.15
  169.6 1.2 copy-start.5
  169.6 1.2 copy-start.13
  171.2 8.9 %collective-permute-start.2 = (bf16[8,16,768]{2,1,0:T(8,128)(2,1)S(1)}, bf16[8,16,768]{2,1,0:T(8,128)(2,1)S(1)}, u32[]{:S(2)}, u32[]{:S(2)}) collective-permute-start(bf16[8,16,768]{2,1,0:T(8,128)(2,1)S(1)} %bitcast.174), channel_id=1, source_target_pairs={{112,0},{0,16},{16,32},{32,48},{48,64},{64,80},{80,96},{96,112},{1... | collective-permute-start | bytes 589832 | tf_op jit(solution)/shard_map/ppermute | solution.py:14
  180.2 7.9 %collective-permute-start.3 = (bf16[32,8,768]{2,1,0:T(8,128)(2,1)S(1)}, bf16[32,8,768]{2,1,0:T(8,128)(2,1)S(1)}, u32[]{:S(2)}, u32[]{:S(2)}) collective-permute-start(bf16[32,8,768]{2,1,0:T(8,128)(2,1)S(1)} %fusion.88), channel_id=1, source_target_pairs={{15,0},{0,1},{1,2},{2,3},{3,4},{4,5},{5,6},{6,7},{7,8},{8,9},{9,10... | collective-permute-start | bytes 1179656 | tf_op jit(solution)/shard_map/ppermute | solution.py:14
  190.6 5.4 copy-start.10
  190.6 6.4 %copy-start.8 = (f32[3,31,31]{2,1,0:T(8,128)S(1)}, f32[3,31,31]{2,1,0:T(8,128)}, u32[]{:S(2)}) copy-start(f32[3,31,31]{2,1,0:T(8,128)} %param.28) | copy-start | bytes 34600
  197.0 234.6 %all-reduce.2.cloned.1.call-start = ((), (), s32[]{:S(2)}) async-start(), calls=%async_computation.2 | async-start | bytes 12582912 | tf_op jit(solution)/shard_map/psum | solution.py:154
  211.1 28.6 %copy-start.18 = (bf16[3,1536,96]{1,2,0:T(8,128)(2,1)S(1)}, bf16[3,1536,96]{1,2,0:T(8,128)(2,1)}, u32[]{:S(2)}) copy-start(bf16[3,1536,96]{1,2,0:T(8,128)(2,1)} %param.26) | copy-start | bytes 2654212
  255.8 1.8 copy-start.19
  268.2 4.7 copy-start.7
  277.3 267.6 %reduce-scatter.4.cloned.1.call-start = ((), (), s32[]{:S(2)}) async-start(), calls=%async_computation.3 | async-start | bytes 6684672
  431.5 4.6 copy-start.2
  436.1 1.8 copy-start.9
  438.0 7.7 %copy-start.16 = (bf16[384,1536]{1,0:T(8,128)(2,1)S(1)}, bf16[384,1536]{1,0:T(8,128)(2,1)}, u32[]{:S(2)}) copy-start(bf16[384,1536]{1,0:T(8,128)(2,1)} %param.32) | copy-start | bytes 3538948
  438.0 7.7 %copy-start.17 = (bf16[1536,384]{1,0:T(8,128)(2,1)S(1)}, bf16[1536,384]{1,0:T(8,128)(2,1)}, u32[]{:S(2)}) copy-start(bf16[1536,384]{1,0:T(8,128)(2,1)} %param.31) | copy-start | bytes 3538948
  468.2 80.5 %copy-start.1 = (bf16[768,2304]{1,0:T(8,128)(2,1)S(1)}, bf16[768,2304]{1,0:T(8,128)(2,1)}, u32[]{:S(2)}) copy-start(bf16[768,2304]{1,0:T(8,128)(2,1)} %param.19) | copy-start | bytes 10616836
  468.2 78.4 %copy-start.11 = (f32[1536]{0:T(1024)S(1)}, f32[1536]{0:T(1024)}, u32[]{:S(2)}) copy-start(f32[1536]{0:T(1024)} %param.33) | copy-start | bytes 18436
Sparse Core Ops, SparseCore 0:
  197.1 42.5 all-gather.1
  277.4 154.0 all-reduce.1
  468.3 76.4 reduce-scatter.3
where the time goes:
time: 560 us; the launch traced here: 555 us
  waiting for transfers between devices  269 us (48%)
  local copies, waits for them, and re-layouts  142 us (25%)
  matrix products  91.1 us (16%)
  other arithmetic  27.1 us (5%)
  between operations  13.8 us (2%)
  starting transfers between devices  12.6 us (2%)
    psum x1, waiting for transfers between devices, per_device(): lax.psum(partial_value.astype(jnp.bfloat16), 'narrow').astype(jnp.float32)  154 us
    add x4, local copies, waits for them, and re-layouts, attend(): score = score * scale[None, :, None, None] + bias[None]  99.5 us
    unnamed x4, waiting for transfers between devices  76.7 us
    dot_general x2, matrix products, attend(): jnp.einsum('nqhd,nkhd->nhqk', query, keys, precision=lax.Precision.HIGHEST)  24.3 us
    all_gather x1, waiting for transfers between devices, per_device(): band_tokens = lax.all_gather(merged, 'narrow', axis=1, tiled=True)  23.5 us
    dot_general x2, matrix products, window_bias(): jnp.einsum('hacq,bdq->habcd', half_rows, onehot, precision=lax.Precision....  21.9 us
    dot_general x1, matrix products, mlp_terms(): jnp.dot(inner_act, w_down, preferred_element_type=jnp.float32)  16.4 us
    ppermute x4, waiting for transfers between devices, from_behind(): return lax.ppermute(block, axis, route)  14.6 us
  transfers between devices with their start and end apart: 7, of which 6 were waited for; matrix products, arithmetic and copies ran while one was open for 23% of the time, Pallas kernels for 0%

commit v1 on v0

v1 whole, which is shorter than its diff:
```python
import functools
import math

import jax
import jax.numpy as jnp
from jax import lax
from jax.experimental import pallas as pl
from jax.experimental.pallas import tpu as pltpu
from jax.sharding import PartitionSpec as P

HD = 32
LOG2E = math.log2(math.e)
MESH = pl.DeviceIdType.MESH
BF = jnp.bfloat16
F32 = jnp.float32
MASK_HI = 144.0
MASK_LO = 100.0 * LOG2E - 144.0
VMEM_LIMIT = 60 << 20


def place():
    wide, narrow = lax.axis_index("wide"), lax.axis_index("narrow")
    return wide, narrow


def shifted(dw, dn):
    wide, narrow = place()
    return (lax.rem(wide + dw + 8, 8), lax.rem(narrow + dn + 16, 16))


def along_x(step):
    wide, narrow = place()
    return (wide, lax.rem(narrow + 4 * step + 16, 16))


def along_y(step):
    wide, narrow = place()
    y = (wide // 4) * 2 + lax.rem(narrow // 2, 2)
    y = lax.rem(y + step + 4, 4)
    return (
        (y // 2) * 4 + lax.rem(wide, 4),
        (narrow // 4) * 4 + lax.rem(y, 2) * 2 + lax.rem(narrow, 2),
    )


def other_core():
    wide, narrow = place()
    return (wide, narrow + 1 - 2 * lax.rem(narrow, 2))


def quad(core, row):
    wide, narrow = place()
    c, r = lax.rem(narrow, 2), lax.rem(narrow // 2, 2)
    c = 1 - c if core else c
    r = 1 - r if row else r
    return (wide, (narrow // 4) * 4 + r * 2 + c)


def greet(sources, expected):
    barrier = pltpu.get_barrier_semaphore()
    for device in sources:
        pl.semaphore_signal(barrier, inc=1, device_id=device, device_id_type=MESH)
    pl.semaphore_wait(barrier, expected)


class Wires:
    def __init__(self, send, recv):
        self.send, self.recv, self.count = send, recv, 0

    def copy(self, src, dst, device):
        i = self.count
        self.count += 1
        out = pltpu.make_async_remote_copy(
            src_ref=src,
            dst_ref=dst,
            send_sem=self.send.at[i],
            recv_sem=self.recv.at[i],
            device_id=device,
            device_id_type=MESH,
        )
        return out

    def go(self, src, dst, device):
        out = self.copy(src, dst, device)
        out.start()
        return out


def dot(a, b):
    return jnp.dot(a, b, preferred_element_type=F32)


def dot_nt(a, b):
    return lax.dot_general(a, b, (((1,), (1,)), ((), ())), preferred_element_type=F32)


def layer_norm(values, gain):
    center = jnp.mean(values, -1, keepdims=True)
    offset = values - center
    spread = jnp.mean(offset * offset, -1, keepdims=True)
    return offset * lax.rsqrt(spread + 1e-05) * gain


def lane_mask(head, last=False):
    lane = lax.broadcasted_iota(jnp.int32, (1, 128), 1)
    keep = lane >= head * HD
    if not last:
        keep = keep & (lane < (head + 1) * HD)
    return jnp.where(keep, 1.0, 0.0)


def head_ones():
    row = lax.rem(lax.broadcasted_iota(jnp.int32, (256, 128), 0), 128) // HD
    col = lax.broadcasted_iota(jnp.int32, (256, 128), 1) // HD
    return jnp.where(row == col, 1.0, 0.0).astype(BF)


def squares_by_head(values, ones):
    square = values * values
    high = square.astype(BF)
    low = (square - high.astype(F32)).astype(BF)
    return dot(jnp.concatenate([high, low], 1), ones)


def bias_tables(rows):
    sub = lax.broadcasted_iota(jnp.int32, (8, 256), 0)
    lane = lax.rem(lax.broadcasted_iota(jnp.int32, (8, 256), 1), 8)
    spread = [jnp.broadcast_to(rows[m : m + 1], (8, 256)) for m in range(4)]
    tables = []
    for m in range(1, 4):
        straight = pltpu.roll(spread[m], 0, 1, stride=1, stride_axis=0)
        around = pltpu.roll(spread[m - 1], 248, 1, stride=1, stride_axis=0)
        tables.append(jnp.where(lane >= sub, straight, around))
    return tables


def bias_block(table, a):
    return pltpu.roll(table, (256 - 8 * (15 - a)) % 256, 1)[:, :128]


def halo_kernel(t_ref, q_ref, r_ref, g_ref, send, recv, local):
    greet(
        [shifted(1, 0), shifted(0, 1), shifted(1, 1), quad(1, 0), quad(0, 1), quad(1, 1)], 6
    )
    w = Wires(send, recv)
    inner = pltpu.make_async_copy(
        t_ref.at[1, pl.ds(64, 192)], r_ref.at[0, pl.ds(0, 192)], local.at[0]
    )
    cps = [
        w.go(t_ref.at[0, pl.ds(64, 192)], r_ref.at[1, pl.ds(0, 192)], shifted(0, -1)),
        w.go(t_ref.at[1, pl.ds(0, 64)], r_ref.at[0, pl.ds(192, 64)], shifted(-1, 0)),
        w.go(t_ref.at[0, pl.ds(0, 64)], r_ref.at[1, pl.ds(192, 64)], shifted(-1, -1)),
    ]
    inner.start()
    cps += [
        w.go(q_ref, g_ref.at[0], quad(1, 0)),
        w.go(q_ref, g_ref.at[1], quad(0, 1)),
        w.go(q_ref, g_ref.at[2], quad(1, 1)),
    ]
    inner.wait()
    for c in cps:
        c.wait()


def halo(tokens, table4):
    any_ = pl.BlockSpec(memory_space=pl.ANY)
    return pl.pallas_call(
        halo_kernel,
        name="halo",
        out_shape=(
            jax.ShapeDtypeStruct((2, 256, 768), BF),
            jax.ShapeDtypeStruct((3, 3, 8, 256), F32),
        ),
        in_specs=[any_, any_],
        out_specs=(any_, any_),
        scratch_shapes=[
            pltpu.SemaphoreType.DMA((6,)),
            pltpu.SemaphoreType.DMA((6,)),
            pltpu.SemaphoreType.DMA((1,)),
        ],
        compiler_params=pltpu.CompilerParams(collective_id=1, has_side_effects=True),
    )(tokens, table4)


def third_kernel(
    x_ref,
    aug_ref,
    tab_ref,
    scale_ref,
    wqkv_ref,
    wproj_ref,
    gain_ref,
    wm_hbm,
    gm_ref,
    o_ref,
    qkv,
    ctx,
    bias,
    flat,
    wm,
    mg,
    sem,
):
    fetch = pltpu.make_async_copy(wm_hbm, wm, sem)
    fetch.start()
    x = x_ref[...].reshape(512, 768)

    def project(n, carry):
        cols = pl.ds(pl.multiple_of(n * 256, 256), 256)
        out = dot(x, wqkv_ref[:, cols]).astype(BF)
        qkv[2 * n] = out[:, :128]
        qkv[2 * n + 1] = out[:, 128:]
        return carry

    lax.fori_loop(0, 9, project, 0)

    ones = head_ones()
    masks = [lane_mask(h).astype(BF) for h in range(4)]
    lane = lax.broadcasted_iota(jnp.int32, (1, 128), 1)
    level = jnp.where(
        lane < 61,
        MASK_HI,
        jnp.where(lane < 64, -MASK_HI, jnp.where(lane < 125, MASK_LO, -MASK_LO)),
    ).astype(BF)

    def group(g, carry):
        for h in range(4):
            tables = bias_tables(tab_ref[4 * g + h])
            for t in range(3):
                for a in range(16):
                    bias[h, t, pl.ds(8 * a, 8), :] = bias_block(tables[t], a)
        scale = scale_ref[g]
        for w in range(2):

            def rows(j):
                return jnp.concatenate(
                    [
                        qkv[6 * j + g, pl.ds(128 * w, 128), :],
                        qkv[6 * j + g, pl.ds(256 + 128 * w, 128), :],
                    ],
                    0,
                )

            q, k, v = rows(0).astype(F32), rows(1).astype(F32), rows(2)
            aug = jnp.concatenate(
                [aug_ref[pl.ds(128 * w, 128), :], aug_ref[pl.ds(256 + 128 * w, 128), :]], 0
            )
            qn = (q * (lax.rsqrt(squares_by_head(q, ones) + 1e-06) * scale)).astype(BF)
            kn = (k * lax.rsqrt(squares_by_head(k, ones) + 1e-06)).astype(BF)
            keys = jnp.concatenate([kn, aug], 1)
            qaug = aug * level
            acc = jnp.zeros((256, 256), F32)
            for h in range(4):
                score = dot_nt(jnp.concatenate([qn * masks[h], qaug], 1), keys)
                middle = bias[h, 1]
                spot = jnp.concatenate(
                    [
                        jnp.concatenate([middle, bias[h, 2]], 1),
                        jnp.concatenate([bias[h, 0], middle], 1),
                    ],
                    0,
                )
                expo = jnp.exp2(score + spot).astype(BF)
                right = jnp.concatenate(
                    [v * masks[h], jnp.broadcast_to(masks[h], (256, 128))], 1
                )
                acc = acc + dot(expo, right)
            out = (acc[:, :128] / acc[:, 128:]).astype(BF)
            cols = pl.ds(pl.multiple_of(g * 128, 128), 128)
            ctx[pl.ds(128 * w, 128), cols] = out[:128]
            ctx[pl.ds(256 + 128 * w, 128), cols] = out[128:]
        return carry

    lax.fori_loop(0, 6, group, 0)

    for half in range(2):
        for part in range(2):
            start = half * 256 + part * 128
            y = dot(ctx[pl.ds(start, 128), :], wproj_ref[...])
            y = layer_norm(y, gain_ref[...]) + x_ref[half, pl.ds(part * 128, 128), :].astype(F32)
            y = y.astype(BF).astype(F32)
            for r in range(16):
                for m in range(6):
                    flat[m, pl.ds((part * 16 + r) * 16 + half * 8, 8), :] = y[
                        8 * r : 8 * r + 8, 128 * m : 128 * m + 128
                    ]

    fetch.wait()
    pieces = []
    for j in range(2):
        side = jnp.concatenate(
            [flat[m, pl.ds(j, 256, stride=2), :] for m in range(6)], 1
        ).reshape(16, 2, 8, 768)
        for i in range(2):
            pieces.append(side[:, i].reshape(128, 768).astype(BF))
    joined = jnp.concatenate(pieces, 1)

    def merge(n, carry):
        cols = pl.ds(pl.multiple_of(n * 256, 256), 256)
        mg[:, cols] = dot(joined, wm[:, cols])
        return carry

    lax.fori_loop(0, 6, merge, 0)
    merged = layer_norm(mg[...], gm_ref[...]).astype(BF)
    row = lax.broadcasted_iota(jnp.int32, (128, 128), 0)
    col = lax.broadcasted_iota(jnp.int32, (128, 128), 1)
    source = lax.rem(row, 64) // 4 * 8 + row // 64 * 4 + lax.rem(row, 4)
    order = jnp.where(col == source, 1.0, 0.0).astype(BF)
    o_ref[...] = dot(order, merged).astype(BF).reshape(2, 64, 1536)


def third(x, aug, tab, scale, wqkv, wproj, gain, wm, gm):
    vm = pl.BlockSpec(memory_space=pltpu.VMEM)
    return pl.pallas_call(
        third_kernel,
        name="third",
        out_shape=jax.ShapeDtypeStruct((2, 64, 1536), BF),
        in_specs=[vm] * 7 + [pl.BlockSpec(memory_space=pl.ANY), vm],
        out_specs=vm,
        scratch_shapes=[
            pltpu.VMEM((18, 512, 128), BF),
            pltpu.VMEM((512, 768), BF),
            pltpu.VMEM((4, 3, 128, 128), F32),
            pltpu.VMEM((6, 512, 128), F32),
            pltpu.VMEM((3072, 1536), BF),
            pltpu.VMEM((128, 1536), F32),
            pltpu.SemaphoreType.DMA,
        ],
        compiler_params=pltpu.CompilerParams(vmem_limit_bytes=VMEM_LIMIT),
        cost_estimate=pl.CostEstimate(
            flops=5_000_000_000, bytes_accessed=16_000_000, transcendentals=3_200_000
        ),
    )(x, aug, tab, scale, wqkv, wproj, gain, wm, gm)


def start_weights(w, weights, gathered):
    flight = []
    for own, (oc, yy, yc) in zip(weights, gathered):
        half = own.shape[0] // 2
        first, second = pl.ds(0, half), pl.ds(half, half)
        a = w.go(own.at[first], yy.at[first], along_y(1))
        b = w.go(own.at[second], yy.at[second], along_y(-1))
        c = w.go(own, oc, other_core())
        flight.append((a, b, c, yy, yc, first, second))
    return flight


def finish_weights(w, flight):
    late = []
    for a, b, c, yy, yc, first, second in flight:
        a.wait_recv()
        late.append(w.go(yy.at[first], yc.at[first], other_core()))
        b.wait_recv()
        late.append(w.go(yy.at[second], yc.at[second], other_core()))
    for a, b, c, *_ in flight:
        a.wait_send()
        b.wait_send()
        c.wait()
    for c in late:
        c.wait()


def gathered_shapes(shapes):
    return tuple(jax.ShapeDtypeStruct(s, BF) for s in shapes for _ in range(3))


def ring_gather(w, blocks):
    right = w.go(blocks.at[0], blocks.at[1], along_x(1))
    left = w.go(blocks.at[0], blocks.at[2], along_x(-1))
    first, second = pl.ds(0, 64), pl.ds(64, 64)
    right.wait_recv()
    on_right = w.go(blocks.at[1, first], blocks.at[3, first], along_x(1))
    yield 1
    left.wait_recv()
    on_left = w.go(blocks.at[2, second], blocks.at[3, second], along_x(-1))
    yield 2
    on_right.wait_recv()
    on_left.wait_recv()
    yield 3
    for c in (right, left, on_right, on_left):
        c.wait_send()


def spread_kernel(m_ref, wa_ref, wp_ref, t_ref, o_ref, *rest):
    gathered, (send, recv, local) = rest[:6], rest[6:]
    greet(
        [
            shifted(0, -1),
            shifted(-1, 0),
            shifted(-1, -1),
            along_x(1),
            along_x(-1),
            along_y(1),
            along_y(-1),
            other_core(),
        ],
        8,
    )
    w = Wires(send, recv)
    inner = pltpu.make_async_copy(
        m_ref.at[0, pl.ds(0, 48)], t_ref.at[0, pl.ds(80, 48)], local.at[0]
    )
    cps = [
        w.go(m_ref.at[1, pl.ds(0, 48)], t_ref.at[0, pl.ds(16, 48)], shifted(0, 1)),
        w.go(m_ref.at[0, pl.ds(48, 16)], t_ref.at[0, pl.ds(64, 16)], shifted(1, 0)),
        w.go(m_ref.at[1, pl.ds(48, 16)], t_ref.at[0, pl.ds(0, 16)], shifted(1, 1)),
    ]
    inner.start()
    flight = start_weights(w, (wa_ref, wp_ref), (gathered[:3], gathered[3:]))
    inner.wait()
    for c in cps:
        c.wait_recv()
    core = [w.copy(t_ref.at[b], o_ref.at[b], other_core()) for b in range(4)]
    core[0].start()
    for b in ring_gather(w, t_ref):
        core[b].start()
    finish_weights(w, flight)
    for c in core:
        c.wait()
    for c in cps:
        c.wait_send()


def spread(merged, wa, wp):
    any_ = pl.BlockSpec(memory_space=pl.ANY)
    n = 3 + 6 + 4 + 4 + 4
    return pl.pallas_call(
        spread_kernel,
        name="spread",
        out_shape=(
            jax.ShapeDtypeStruct((4, 128, 1536), BF),
            jax.ShapeDtypeStruct((4, 128, 1536), BF),
        )
        + gathered_shapes([wa.shape, wp.shape]),
        in_specs=[any_] * 3,
        out_specs=(any_,) * 8,
        scratch_shapes=[
            pltpu.SemaphoreType.DMA((n,)),
            pltpu.SemaphoreType.DMA((n,)),
            pltpu.SemaphoreType.DMA((1,)),
        ],
        compiler_params=pltpu.CompilerParams(collective_id=2, has_side_effects=True),
    )(merged, wa, wp)


def fourth_kernel(
    t_ref, o_ref, tab_ref, w0, w1, w2, w3, p0, p1, p2, p3, part_ref, own_ref, bias, wp, qkv
):
    core = lax.rem(lax.axis_index("narrow"), 2)
    for s, p in enumerate((p0, p1, p2, p3)):
        wp[pl.ds(128 * s, 96), :] = p[...]
        wp[pl.ds(128 * s + 96, 32), :] = jnp.zeros((32, 1536), BF)

    def build(n, carry):
        rows = tab_ref[n]
        tables = bias_tables(rows)
        side = jnp.where(core == 0, tables[2], tables[0])
        for a in range(16):
            bias[n, pl.ds(8 * a, 8), pl.ds(0, 128)] = bias_block(tables[1], a)
            bias[n, pl.ds(8 * a, 8), pl.ds(128, 128)] = bias_block(side, a)
        return carry

    lax.fori_loop(0, 12, build, 0)
    ones = head_ones()
    masks = [lane_mask(h, h == 2).astype(BF) for h in range(3)]
    row = lax.broadcasted_iota(jnp.int32, (128, 128), 0)
    col = lax.broadcasted_iota(jnp.int32, (128, 128), 1)
    source = lax.rem(row, 8) // 4 * 64 + row // 8 * 4 + lax.rem(row, 4)
    order = jnp.where(col == source, 1.0, 0.0).astype(BF)

    def block(b, carry):
        mine = dot(order, t_ref[b]).astype(BF)
        theirs = dot(order, o_ref[b]).astype(BF)

        @pl.when(b == 0)
        def _():
            own_ref[...] = mine

        both = jnp.concatenate([mine, theirs], 0)
        outs = []
        for s, wa in enumerate((w0, w1, w2, w3)):
            qkv[...] = dot(both, wa[...]).astype(BF)
            q = qkv[pl.ds(0, 128), pl.ds(0, 128)].astype(F32)
            k = qkv[:, pl.ds(128, 128)].astype(F32)
            v = qkv[:, pl.ds(256, 128)]
            scale = tab_ref[3 * s, 5:6, :128]
            qn = (q * (lax.rsqrt(squares_by_head(q, ones) + 1e-06) * scale)).astype(BF)
            kn = (k * lax.rsqrt(squares_by_head(k, ones) + 1e-06)).astype(BF)
            acc = jnp.zeros((128, 256), F32)
            for h in range(3):
                score = dot_nt(qn * masks[h], kn)
                expo = jnp.exp2(score + bias[3 * s + h]).astype(BF)
                right = jnp.concatenate(
                    [v * masks[h], jnp.broadcast_to(masks[h], (256, 128))], 1
                )
                acc = acc + dot(expo, right)
            outs.append((acc[:, :128] / acc[:, 128:]).astype(BF))
        part_ref[b] = dot(jnp.concatenate(outs, 1), wp[...]).astype(BF)
        return carry

    lax.fori_loop(0, 4, block, 0)


def fourth(t, o, tab, was, wps):
    vm = pl.BlockSpec(memory_space=pltpu.VMEM)
    return pl.pallas_call(
        fourth_kernel,
        name="fourth",
        out_shape=(
            jax.ShapeDtypeStruct((4, 128, 1536), BF),
            jax.ShapeDtypeStruct((128, 1536), BF),
        ),
        in_specs=[vm] * 11,
        out_specs=(vm, vm),
        scratch_shapes=[
            pltpu.VMEM((12, 128, 256), F32),
            pltpu.VMEM((512, 1536), BF),
            pltpu.VMEM((256, 384), BF),
        ],
        compiler_params=pltpu.CompilerParams(vmem_limit_bytes=VMEM_LIMIT),
    )(t, o, tab, *was, *wps)


def ring_sum(w, part, buf):
    first, second = pl.ds(0, 64), pl.ds(64, 64)
    far_right = w.go(part.at[3, first], buf.at[0], along_x(1))
    far_left = w.go(part.at[3, second], buf.at[1], along_x(-1))
    near_right = w.go(part.at[2, second], buf.at[2], along_x(1))
    near_left = w.go(part.at[1, first], buf.at[3], along_x(-1))
    far_right.wait_recv()
    part[2, first, :] = (part[2, first, :].astype(F32) + buf[0].astype(F32)).astype(BF)
    last_right = w.go(part.at[2, first], buf.at[4], along_x(1))
    far_left.wait_recv()
    part[1, second, :] = (part[1, second, :].astype(F32) + buf[1].astype(F32)).astype(BF)
    last_left = w.go(part.at[1, second], buf.at[5], along_x(-1))
    near_right.wait_recv()
    near_left.wait_recv()
    last_right.wait_recv()
    last_left.wait_recv()
    top = part[0, first, :].astype(F32) + buf[4].astype(F32) + buf[3].astype(F32)
    low = part[0, second, :].astype(F32) + buf[2].astype(F32) + buf[5].astype(F32)
    for c in (far_right, far_left, near_right, near_left, last_right, last_left):
        c.wait_send()
    return jnp.concatenate([top, low], 0)


def middle_kernel(p_ref, own_ref, gain_ref, wu_ref, wd_ref, h_ref, *rest):
    gathered, (part, buf, send, recv, local) = rest[:6], rest[6:]
    greet([along_x(1), along_x(-1), along_y(1), along_y(-1), other_core()], 5)
    w = Wires(send, recv)
    take = pltpu.make_async_copy(p_ref, part, local.at[0])
    take.start()
    flight = start_weights(w, (wu_ref, wd_ref), (gathered[:3], gathered[3:]))
    take.wait()
    total = ring_sum(w, part, buf)
    h_ref[0] = (own_ref[...].astype(F32) + layer_norm(total, gain_ref[...])).astype(BF)
    for _ in ring_gather(w, h_ref):
        pass
    finish_weights(w, flight)


def middle(part, own, gain, wu, wd):
    any_ = pl.BlockSpec(memory_space=pl.ANY)
    vm = pl.BlockSpec(memory_space=pltpu.VMEM)
    n = 6 + 6 + 4 + 4
    return pl.pallas_call(
        middle_kernel,
        name="middle",
        out_shape=(jax.ShapeDtypeStruct((4, 128, 1536), BF),)
        + gathered_shapes([wu.shape, wd.shape]),
        in_specs=[any_, vm, vm, any_, any_],
        out_specs=(vm,) + (any_,) * 6,
        scratch_shapes=[
            pltpu.VMEM((4, 128, 1536), BF),
            pltpu.VMEM((6, 64, 1536), BF),
            pltpu.SemaphoreType.DMA((n,)),
            pltpu.SemaphoreType.DMA((n,)),
            pltpu.SemaphoreType.DMA((1,)),
        ],
        compiler_params=pltpu.CompilerParams(
            collective_id=3, has_side_effects=True, vmem_limit_bytes=VMEM_LIMIT
        ),
    )(part, own, gain, wu, wd)


def last_kernel(p_ref, h_ref, gain_ref, out_ref, part, buf, send, recv, local):
    greet([along_x(1), along_x(-1)], 2)
    w = Wires(send, recv)
    take = pltpu.make_async_copy(p_ref, part, local.at[0])
    take.start()
    take.wait()
    total = ring_sum(w, part, buf)
    out_ref[...] = (h_ref[0].astype(F32) + layer_norm(total, gain_ref[...])).astype(BF)


def last(part, hidden, gain):
    any_ = pl.BlockSpec(memory_space=pl.ANY)
    vm = pl.BlockSpec(memory_space=pltpu.VMEM)
    return pl.pallas_call(
        last_kernel,
        name="last",
        out_shape=jax.ShapeDtypeStruct((128, 1536), BF),
        in_specs=[any_, vm, vm],
        out_specs=vm,
        scratch_shapes=[
            pltpu.VMEM((4, 128, 1536), BF),
            pltpu.VMEM((6, 64, 1536), BF),
            pltpu.SemaphoreType.DMA((6,)),
            pltpu.SemaphoreType.DMA((6,)),
            pltpu.SemaphoreType.DMA((1,)),
        ],
        compiler_params=pltpu.CompilerParams(
            collective_id=4, has_side_effects=True, vmem_limit_bytes=VMEM_LIMIT
        ),
    )(part, hidden, gain)


def gelu(x):
    return 0.5 * x * (1.0 + lax.erf(x * (2.0**-0.5)))


def mlp_kernel(h_ref, u0, u1, u2, u3, d0, d1, d2, d3, part_ref, acc):
    h = h_ref[...].reshape(512, 1536)
    for s, (wu, wd) in enumerate(((u0, d0), (u1, d1), (u2, d2), (u3, d3))):
        inner = gelu(dot(h, wu[...])).astype(BF)

        def down(n, carry):
            cols = pl.ds(pl.multiple_of(n * 256, 256), 256)
            term = dot(inner, wd[:, cols])
            if s > 0:
                term = term + acc[:, cols]
            if s < 3:
                acc[:, cols] = term
            else:
                part_ref[:, :, cols] = term.astype(BF).reshape(4, 128, 256)
            return carry

        lax.fori_loop(0, 6, down, 0)


def mlp(hidden, wus, wds):
    vm = pl.BlockSpec(memory_space=pltpu.VMEM)
    return pl.pallas_call(
        mlp_kernel,
        name="mlp",
        out_shape=jax.ShapeDtypeStruct((4, 128, 1536), BF),
        in_specs=[vm] * 9,
        out_specs=vm,
        scratch_shapes=[pltpu.VMEM((512, 1536), F32)],
        compiler_params=pltpu.CompilerParams(vmem_limit_bytes=VMEM_LIMIT),
    )(hidden, *wus, *wds)


def table_rows(table):
    heads = table.shape[0]
    values = 16.0 * LOG2E * jax.nn.sigmoid(table[:, ::-1, ::-1])
    values = jnp.pad(values, ((0, 0), (0, 1), (1, 0)))
    values = values.reshape(heads, 32, 4, 8).transpose(0, 2, 1, 3).reshape(heads, 4, 256)
    return jnp.pad(values, ((0, 0), (0, 4), (0, 0)))


def per_device(
    tokens,
    regions,
    w_qkv3,
    w_proj3,
    bias_table3,
    logit_scale3,
    gain_attn3,
    w_merge,
    gain_merge,
    w_qkv4,
    w_proj4,
    bias_table4,
    logit_scale4,
    gain_attn4,
    w_up4,
    w_down4,
    gain_mlp4,
):
    halves = tokens.reshape(32, 2, 8, 768).transpose(1, 0, 2, 3).reshape(2, 256, 768)
    tab4 = table_rows(bias_table4)
    scale4 = jnp.pad(jnp.repeat(logit_scale4 * LOG2E, HD), (0, 160))
    tab4 = tab4.at[0, 5].set(scale4)
    rolled, tabs = halo(halves, tab4)

    labels = regions.reshape(32, 2, 8).transpose(1, 0, 2).reshape(512, 1)
    lane = jnp.arange(128)[None, :]
    aug = (labels == lane) | (labels + 64 == lane) | (lane == 61) | (lane == 125)
    scale3 = jnp.repeat(logit_scale3 * LOG2E, HD).reshape(6, 1, 128)
    merged = third(
        rolled,
        aug.astype(BF),
        table_rows(bias_table3),
        scale3,
        w_qkv3,
        w_proj3,
        gain_attn3[None],
        w_merge,
        gain_merge[None],
    )
    wa = jnp.pad(w_qkv4, ((0, 0), (0, 0), (0, 32))).transpose(1, 0, 2).reshape(1536, 384)
    t, o, *gathered = spread(merged, wa, w_proj4)
    tab_all = jnp.concatenate([tab4[None], tabs], 0).reshape(12, 8, 256)
    part, own = fourth(t, o, tab_all, [wa] + gathered[:3], [w_proj4] + gathered[3:])
    hidden, *gathered = middle(part, own, gain_attn4[None], w_up4, w_down4)
    part = mlp(hidden, [w_up4] + gathered[:3], [w_down4] + gathered[3:])
    out = last(part, hidden, gain_mlp4[None])
    return out.reshape(16, 8, 1536)


def solution(mesh):
    placed = (
        P("wide", "narrow", None),
        P("wide", "narrow"),
        P(),
        P(),
        P(),
        P(),
        P(),
        P(),
        P(),
        P(None, None, "narrow"),
        P("narrow", None),
        P("narrow", None, None),
        P("narrow"),
        P(),
        P(None, "narrow"),
        P("narrow", None),
        P(),
    )
    return jax.shard_map(
        per_device, mesh=mesh, in_specs=placed, out_specs=P("wide", "narrow", None), check_vma=False
    )
```

time: 560 us -> 193 us (0.34)
  waiting for transfers between devices: 269 us -> 0 us
  Pallas kernels: 0 us -> 173 us
  local copies, waits for them, and re-layouts: 142 us -> 12.8 us
  matrix products: 91.1 us -> 0 us
  other arithmetic: 27.1 us -> 6.43 us
  between operations: 13.8 us -> 0.25 us
  starting transfers between devices: 12.6 us -> 0 us
    pallas_call x0 -> x7, Pallas kernels: none -> 173 us  [the longest x1 41.9 us: middle(): pl.pallas_call(middle_kernel, name='middle', out_shape=(jax.ShapeDtypeStr...]
    psum x1 -> x0, waiting for transfers between devices: 154 us -> none  [per_device(): lax.psum(partial_value.astype(jnp.bfloat16), 'narrow').astype(jnp.float32)]
    add x4 -> x0, local copies, waits for them, and re-layouts: 99.5 us -> none  [attend(): score = score * scale[None, :, None, None] + bias[None]]
    dot_general x14 -> x0, matrix products: 91.1 us -> none  [the longest x2 24.3 us: attend(): jnp.einsum('nqhd,nkhd->nhqk', query, keys, precision=lax.Precision.HIGHEST)]
    unnamed x4 -> x0, waiting for transfers between devices: 76.7 us -> none
    all_gather x1 -> x0, waiting for transfers between devices: 23.5 us -> none  [per_device(): band_tokens = lax.all_gather(merged, 'narrow', axis=1, tiled=True)]
    ppermute x4 -> x0, waiting for transfers between devices: 14.6 us -> none  [from_behind(): return lax.ppermute(block, axis, route)]
    ppermute x4 -> x0, starting transfers between devices: 12.6 us -> none  [from_behind(): return lax.ppermute(block, axis, route)]
  transfers between devices with their start and end apart: 7 -> 0, of which waited for: 6 -> 0; matrix products, arithmetic and copies ran while one was open for 23% -> 0% of each run, Pallas kernels for 0% -> 0%
where the time goes in v1:
time: 193 us
  Pallas kernels  173 us (90%)
  local copies, waits for them, and re-layouts  12.8 us (7%)
  other arithmetic  6.43 us (3%)
    pallas_call x1, Pallas kernels, middle(): pl.pallas_call(middle_kernel, name='middle', out_shape=(jax.ShapeDtypeStr...  41.9 us
    pallas_call x1, Pallas kernels, spread(): pl.pallas_call(spread_kernel, name='spread', out_shape=(jax.ShapeDtypeStr...  32.7 us
    pallas_call x1, Pallas kernels, fourth(): pl.pallas_call(fourth_kernel, name='fourth', out_shape=(jax.ShapeDtypeStr...  24.8 us
    pallas_call x1, Pallas kernels, last(): pl.pallas_call(last_kernel, name='last', out_shape=jax.ShapeDtypeStruct((...  20.3 us
    pallas_call x1, Pallas kernels, third(): pl.pallas_call(third_kernel, name='third', out_shape=jax.ShapeDtypeStruct...  19.2 us
    pallas_call x1, Pallas kernels, halo(): pl.pallas_call(halo_kernel, name='halo', out_shape=(jax.ShapeDtypeStruct(...  18 us
    pallas_call x1, Pallas kernels, mlp(): pl.pallas_call(mlp_kernel, name='mlp', out_shape=jax.ShapeDtypeStruct((4,...  16.4 us

profile of v1, /device:TPU:1, one launch (start us, length us, event | category | flops | bytes accessed | tf_op | source)
XLA Modules:
  0.0 192.7 jit_solution(15675460523157538628)
XLA Ops:
  0.0 0.6 fusion.4
  0.6 0.9 copy.23
  1.5 0.1 rev.6
  1.7 0.1 copy.24
  1.8 0.1 reshape.100
  1.9 1.4 and_reduce_fusion
  3.3 0.7 broadcast_multiply_fusion.1
  4.1 1.8 broadcast_select_fusion
  6.0 1.2 scatter.4.q_ref
  7.3 1.0 copy_bitcast_fusion.t_ref
  8.2 18.0 %halo.1 = (bf16[2,256,768]{2,1,0:T(8,128)(2,1)}, f32[3,3,8,256]{3,2,1,0:T(8,128)}) custom-call(bf16[2,256,768]{2,1,0:T(8,128)(2,1)} %copy_bitcast_fusion.t_ref, f32[3,8,256]{2,1,0:T(8,128)} %copy-done.3), custom_call_target="tpu_custom_call" | custom-call | tf_op jit(solution)/shard_map/halo/pallas_call | solution.py:167
  26.2 1.5 pad_maximum_fusion
  27.9 0.9 fusion.3.aug_ref
  28.8 0.3 copy.26
  29.1 0.4 rev.7
  29.4 0.1 divide_multiply_fusion
  29.7 0.3 copy.27
  30.0 0.2 copy.28
  30.2 0.7 pad.31.tab_ref
  31.0 0.7 broadcast_in_dim.29.scale_ref
  31.7 0.6 broadcast_in_dim.31.gm_ref
  32.3 0.6 broadcast_in_dim.30.gain_ref
  32.9 19.2 %third.1.m_ref = bf16[2,64,1536]{2,1,0:T(8,128)(2,1)} custom-call(bf16[2,256,768]{2,1,0:T(8,128)(2,1)} %get-tuple-element.36.x_ref, bf16[512,128]{1,0:T(8,128)(2,1)} %fusion.3.aug_ref, f32[24,8,256]{2,1,0:T(8,128)} %pad.31.tab_ref, f32[6,1,128]{2,1,0:T(1,128)} %broadcast_in_dim.29.scale_ref, bf16[768,2304]{1,0:T(8,128)(2,1)} %wqkv_ref.1, ...), custom_call_target="tpu_custom_call" | custom-call | flops 5000000000 | bytes 16000000 | tf_op jit(solution)/shard_map/third/pallas_call | solution.py:314
  52.3 1.4 copy.29.wa_ref.w0
  53.7 32.7 %spread.1 = (bf16[4,128,1536]{2,1,0:T(8,128)(2,1)}, bf16[4,128,1536]{2,1,0:T(8,128)(2,1)}, bf16[1536,384]{1,0:T(8,128)(2,1)}, bf16[1536,384]{1,0:T(8,128)(2,1)},...) custom-call(bf16[2,64,1536]{2,1,0:T(8,128)(2,1)} %third.1.m_ref, ...), custom_call_target="tpu_custom_call" | custom-call | tf_op jit(solution)/shard_map/spread/pallas_call | solution.py:427
  86.4 24.8 %fourth.1 = (bf16[4,128,1536]{2,1,0:T(8,128)(2,1)}, bf16[128,1536]{1,0:T(8,128)(2,1)}) custom-call(bf16[4,128,1536]{2,1,0:T(8,128)(2,1)} %get-tuple-element.37.t_ref, bf16[4,128,1536]{2,1,0:T(8,128)(2,1)} %get-tuple-element.38.o_ref, f32[12,8,256]{2,1,0:T(8,128)} %bitcast.32, bf16[1536,384]{1,0:T(8,128)(2,1)} %copy.29.wa_ref.w0, ...), custom_call_target="tpu_custom_call" | custom-call | tf_op jit(solution)/shard_map/fourth/pallas_call | solution.py:506
  111.2 0.6 broadcast_in_dim.33.gain_ref
  111.8 41.9 %middle.1 = (bf16[4,128,1536]{2,1,0:T(8,128)(2,1)}, bf16[1536,384]{1,0:T(8,128)(2,1)}, bf16[1536,384]{1,0:T(8,128)(2,1)}, bf16[1536,384]{1,0:T(8,128)(2,1)}, bf1...) custom-call(bf16[4,128,1536]{2,1,0:T(8,128)(2,1)} %get-tuple-element.46.p_ref, ...), custom_call_target="tpu_custom_call" | custom-call | tf_op jit(solution)/shard_map/middle/pallas_call | solution.py:566
  153.7 16.4 %mlp.1.p_ref = bf16[4,128,1536]{2,1,0:T(8,128)(2,1)} custom-call(bf16[4,128,1536]{2,1,0:T(8,128)(2,1)} %get-tuple-element.48.h_ref, bf16[1536,384]{1,0:T(8,128)(2,1)} %u0.1, bf16[1536,384]{1,0:T(8,128)(2,1)} %get-tuple-element.49.u1, bf16[1536,384]{1,0:T(8,128)(2,1)} %get-tuple-element.50.u2, bf16[1536,384]{1,0:T(8,128)(2,1)} %get-tuple-element.51.u3, ...), custom_call_target="tpu_custom_call" | custom-call | tf_op jit(solution)/shard_map/mlp/pallas_call | solution.py:643
  170.1 0.6 broadcast_in_dim.34.gain_ref
  170.7 20.3 %last.1 = bf16[128,1536]{1,0:T(8,128)(2,1)} custom-call(bf16[4,128,1536]{2,1,0:T(8,128)(2,1)} %mlp.1.p_ref, bf16[4,128,1536]{2,1,0:T(8,128)(2,1)} %get-tuple-element.48.h_ref, f32[1,1536]{1,0:T(1,128)} %broadcast_in_dim.34.gain_ref), custom_call_target="tpu_custom_call" | custom-call | tf_op jit(solution)/shard_map/last/pallas_call | solution.py:599
  190.9 1.8 copy.34
  (36 shorter events, 0.7 us)
Async XLA Ops:
  0.0 7.2 %copy-start = (bf16[32,16,768]{2,1,0:T(8,128)(2,1)S(1)}, bf16[32,16,768]{2,1,0:T(8,128)(2,1)}, u32[]{:S(2)}) copy-start(bf16[32,16,768]{2,1,0:T(8,128)(2,1)} %param.19) | copy-start | bytes 2359300
  7.2 1.0 copy-start.3
  7.2 20.5 %copy-start.4 = (s32[32,16]{0,1:T(8,128)S(1)}, s32[32,16]{0,1:T(8,128)}, u32[]{:S(2)}) copy-start(s32[32,16]{0,1:T(8,128)} %param.20) | copy-start | bytes 6148
  7.2 21.6 %copy-start.2 = (f32[24,31,31]{2,0,1:T(8,128)S(1)}, f32[24,31,31]{2,0,1:T(8,128)}, u32[]{:S(2)}) copy-start(f32[24,31,31]{2,0,1:T(8,128)} %param.23) | copy-start | bytes 276772
  29.6 1.3 copy-start.9
  29.6 2.2 %copy-start.5 = (f32[1536]{0:T(1024)S(1)}, f32[1536]{0:T(1024)}, u32[]{:S(2)}) copy-start(f32[1536]{0:T(1024)} %param.27) | copy-start | bytes 18436
  29.6 2.7 %copy-start.8 = (f32[768]{0:T(1024)S(1)}, f32[768]{0:T(1024)}, u32[]{:S(2)}) copy-start(f32[768]{0:T(1024)} %param.25) | copy-start | bytes 9220
  32.9 19.2 %copy-start.1 = (bf16[3,1536,96]{1,2,0:T(8,128)(2,1)S(1)}, bf16[3,1536,96]{1,2,0:T(8,128)(2,1)}, u32[]{:S(2)}) copy-start(bf16[3,1536,96]{1,2,0:T(8,128)(2,1)} %param.28) | copy-start | bytes 2654212
  86.4 24.8 %copy-start.6 = (f32[1536]{0:T(1024)S(1)}, f32[1536]{0:T(1024)}, u32[]{:S(2)}) copy-start(f32[1536]{0:T(1024)} %param.32) | copy-start | bytes 18436
  153.7 16.4 %copy-start.7 = (f32[1536]{0:T(1024)S(1)}, f32[1536]{0:T(1024)}, u32[]{:S(2)}) copy-start(f32[1536]{0:T(1024)} %param.35) | copy-start | bytes 18436

commit v2 on v0

v2 whole, which is shorter than its diff:
```python
import jax
import jax.numpy as jnp
from jax import lax
from jax.experimental import pallas as pl
from jax.experimental.pallas import tpu as pltpu
from jax.sharding import PartitionSpec as P

HD = 32
MESH = pl.DeviceIdType.MESH
BF = jnp.bfloat16
F32 = jnp.float32
MASK = 100.0
WIRES = 64
VMEM_LIMIT = 60 << 20


def place():
    wide, narrow = lax.axis_index("wide"), lax.axis_index("narrow")
    return wide, narrow


def shifted(dw, dn):
    wide, narrow = place()
    return (lax.rem(wide + dw + 8, 8), lax.rem(narrow + dn + 16, 16))


def along_x(step):
    wide, narrow = place()
    return (wide, lax.rem(narrow + 4 * step + 16, 16))


def along_y(step):
    wide, narrow = place()
    y = (wide // 4) * 2 + lax.rem(narrow // 2, 2)
    y = lax.rem(y + step + 4, 4)
    return (
        (y // 2) * 4 + lax.rem(wide, 4),
        (narrow // 4) * 4 + lax.rem(y, 2) * 2 + lax.rem(narrow, 2),
    )


def other_core():
    wide, narrow = place()
    return (wide, narrow + 1 - 2 * lax.rem(narrow, 2))


def quad(core, row):
    wide, narrow = place()
    c, r = lax.rem(narrow, 2), lax.rem(narrow // 2, 2)
    c = 1 - c if core else c
    r = 1 - r if row else r
    return (wide, (narrow // 4) * 4 + r * 2 + c)


def greet(sources, expected):
    barrier = pltpu.get_barrier_semaphore()
    for device in sources:
        pl.semaphore_signal(barrier, inc=1, device_id=device, device_id_type=MESH)
    pl.semaphore_wait(barrier, expected)


class Wires:
    def __init__(self, send, recv):
        self.send, self.recv, self.count = send, recv, 0

    def copy(self, src, dst, device):
        i = self.count
        self.count += 1
        out = pltpu.make_async_remote_copy(
            src_ref=src,
            dst_ref=dst,
            send_sem=self.send.at[i],
            recv_sem=self.recv.at[i],
            device_id=device,
            device_id_type=MESH,
        )
        return out

    def go(self, src, dst, device):
        out = self.copy(src, dst, device)
        out.start()
        return out


def dot(a, b):
    return jnp.dot(a, b, preferred_element_type=F32)


def dot_nt(a, b):
    return lax.dot_general(a, b, (((1,), (1,)), ((), ())), preferred_element_type=F32)


def iota(shape, axis):
    return lax.broadcasted_iota(jnp.int32, shape, axis)


def layer_norm(values, gain):
    center = jnp.mean(values, -1, keepdims=True)
    offset = values - center
    spread = jnp.mean(offset * offset, -1, keepdims=True)
    return offset * lax.rsqrt(spread + 1e-05) * gain


def gelu(x):
    return 0.5 * x * (1.0 + lax.erf(x * (2.0**-0.5)))


def head_blocks():
    same = iota((256, 256), 0) // HD == iota((256, 256), 1) // HD
    return jnp.where(same, 1.0, 0.0).astype(BF)


def inverse_norms(values, blocks):
    return lax.rsqrt(dot((values * values).astype(BF), blocks) + 1e-06)


def lane_pick(values):
    lane = iota((1, 128), 1)
    out = values[0]
    for h in range(1, len(values)):
        out = jnp.where(lane >= h * HD, values[h], out)
    return out


def head_masks(count):
    lane = iota((1, 128), 1) // HD
    return [jnp.where(lane == h, 1.0, 0.0).astype(BF) for h in range(count)]


def table_rows(tables):
    lane = iota((256, 1024), 1)
    spot = lax.rem(iota((256, 1024), 0), 128)
    pick = jnp.where(spot == 31 - 8 * (lane // 256) - lax.rem(lane, 8), 1.0, 0.0).astype(BF)
    high = tables.astype(BF)
    low = (tables - high.astype(F32)).astype(BF)
    moved = dot(jnp.concatenate([high, low], 1), pick)
    row = lax.rem(iota(moved.shape, 0), 32)
    f = lax.rem(iota(moved.shape, 1), 256) // 8
    return jnp.where(row == 30 - f, moved, 0.0)


def head_row(moved, head):
    values = jnp.sum(moved[32 * head : 32 * head + 32], 0, keepdims=True)
    return 16.0 / (1.0 + jnp.exp(-values))


def bias_tables(rows):
    sub = iota((8, 256), 0)
    lane = lax.rem(iota((8, 256), 1), 8)
    spread = [jnp.broadcast_to(r, (8, 256)) for r in rows]
    tables = []
    for m in range(1, 4):
        straight = pltpu.roll(spread[m], 0, 1, stride=1, stride_axis=0)
        around = pltpu.roll(spread[m - 1], 248, 1, stride=1, stride_axis=0)
        tables.append(jnp.where(lane >= sub, straight, around))
    return tables


def bias_block(table, a):
    return pltpu.roll(table, (256 - 8 * (15 - a)) % 256, 1)[:, :128]


def whole_kernel(
    tokens_ref,
    small_ref,
    scale3_ref,
    scale4_ref,
    wqkv3_hbm,
    wproj3_hbm,
    gain_attn3,
    wm_hbm,
    gain_merge,
    wqkv4_hbm,
    wproj4_hbm,
    gain_attn4,
    wup_hbm,
    wdown_hbm,
    gain_mlp4,
    out_ref,
    ctx,
    xs,
    xr,
    aug,
    wqkv,
    wproj,
    wm,
    qkv,
    bias3,
    flat,
    m4,
    back,
    tabs,
    bias4,
    wtmp,
    wa,
    wp,
    blocks,
    others,
    qkv4,
    part,
    buf4,
    bufm,
    hidden,
    wu,
    wd,
    send,
    recv,
    local,
):
    w = Wires(send, recv)
    core = lax.rem(lax.axis_index("narrow"), 2)
    first, second = pl.ds(0, 64), pl.ds(64, 64)

    loads = []
    for i, (src, dst) in enumerate(
        (
            (tokens_ref, ctx),
            (wqkv4_hbm, wtmp),
            (wproj4_hbm, wp.at[0, pl.ds(0, 96)]),
            (wqkv3_hbm, wqkv),
            (wproj3_hbm, wproj),
            (wm_hbm, wm),
            (wup_hbm, wu.at[:, pl.ds(0, 384)]),
            (wdown_hbm, wd.at[pl.ds(0, 384)]),
        )
    ):
        load = pltpu.make_async_copy(src, dst, local.at[i])
        load.start()
        loads.append(load)
    get_tokens, get_qkv4, get_proj4, get_qkv3, get_proj3, get_merge, get_up, get_down = loads

    partners = [shifted(i, j) for i, j in ((0, 1), (1, 0), (1, 1), (0, -1), (-1, 0), (-1, -1))]
    partners += [quad(1, 0), quad(0, 1), quad(1, 1), along_x(1), along_x(-1), along_x(2)]
    partners += [along_y(1), along_y(-1)]
    greet(partners, len(partners))

    get_tokens.wait()
    grouped = ctx[...].astype(F32).reshape(32, 2, 8, 768)
    for half in range(2):
        xs[half] = grouped[:, half].reshape(256, 768).astype(BF)
    halo = [
        w.go(xs.at[0, pl.ds(64, 192)], xr.at[1, pl.ds(0, 192)], shifted(0, -1)),
        w.go(xs.at[1, pl.ds(0, 64)], xr.at[0, pl.ds(192, 64)], shifted(-1, 0)),
        w.go(xs.at[0, pl.ds(0, 64)], xr.at[1, pl.ds(192, 64)], shifted(-1, -1)),
    ]
    xr[0, pl.ds(0, 192), :] = xs[1, pl.ds(64, 192), :]

    get_qkv4.wait()
    for j in range(3):
        wa[:, pl.ds(128 * j, 128)] = jnp.concatenate(
            [wtmp[j].astype(F32), jnp.zeros((1536, 32), F32)], 1
        ).astype(BF)
    get_proj4.wait()
    for s in range(4):
        wp[s, pl.ds(96, 32), :] = jnp.zeros((32, 1536), BF)

    def column(s):
        return pl.ds(384 * s, 384)

    def both_ways(own, away, cut):
        up, down = pl.ds(0, cut), pl.ds(cut, cut)
        return (
            w.go(own(0, up), away(2, up), along_y(1)),
            w.go(own(0, down), away(2, down), along_y(-1)),
            w.go(own(0, pl.ds(0, 2 * cut)), away(1, pl.ds(0, 2 * cut)), other_core()),
        )

    def pass_on(piece, cut, flight):
        up, down = pl.ds(0, cut), pl.ds(cut, cut)
        flight[0].wait_recv()
        a = w.go(piece(2, up), piece(3, up), other_core())
        flight[1].wait_recv()
        b = w.go(piece(2, down), piece(3, down), other_core())
        return a, b

    def piece_a(s, rows):
        return wa.at[rows, column(s)]

    def piece_p(s, rows):
        return wp.at[s, rows]

    def piece_u(s, rows):
        return wu.at[rows, column(s)]

    def piece_d(s, rows):
        return wd.at[pl.ds(384 * s + rows.start, rows.size)]

    flight_a = both_ways(piece_a, piece_a, 768)
    flight_p = both_ways(piece_p, piece_p, 48)

    moved = table_rows(small_ref[pl.ds(24, 3)].reshape(96, 128))
    lane = iota((1, 256), 1)
    for h in range(3):
        row = head_row(moved, h)
        for m in range(4):
            tabs[0, h, pl.ds(m, 1), :] = row[:, 256 * m : 256 * m + 256]
    tabs[0, 0, pl.ds(4, 1), :] = jnp.where(
        lane < HD, scale4_ref[0], jnp.where(lane < 2 * HD, scale4_ref[1], scale4_ref[2])
    )
    flight_t = [
        w.go(tabs.at[0], tabs.at[1], quad(1, 0)),
        w.go(tabs.at[0], tabs.at[2], quad(0, 1)),
        w.go(tabs.at[0], tabs.at[3], quad(1, 1)),
    ]

    token = iota((512, 32), 0)
    rows = jnp.where(lax.rem(token, 256) // 8 == iota((512, 32), 1), 1.0, 0.0).astype(BF)
    labels = dot(rows, small_ref[27].astype(BF))
    token = iota((512, 128), 0)
    at = iota((512, 128), 1)
    labels = jnp.where(at == token // 256 * 8 + lax.rem(token, 8), labels, 0.0).astype(BF)
    labels = dot(labels, jnp.ones((128, 128), BF))
    aug[...] = jnp.where((labels == at.astype(F32)) | (at == 64), 1.0, 0.0).astype(BF)

    def build3(g, carry):
        moved = table_rows(small_ref[pl.ds(4 * g, 4)].reshape(128, 128))
        for h in range(4):
            row = head_row(moved, h)
            tables = bias_tables([row[:, 256 * m : 256 * m + 256] for m in range(4)])
            for t in range(3):
                for a in range(16):
                    bias3[4 * g + h, t, pl.ds(8 * a, 8), :] = bias_block(tables[t], a)
        return carry

    lax.fori_loop(0, 6, build3, 0)

    get_qkv3.wait()
    for c in halo:
        c.wait_recv()
    x = xr[...].reshape(512, 768)
    square = head_blocks()
    lane = iota((1, 256), 1) // HD
    for j in range(3):
        out = dot(x, wqkv[:, pl.ds(768 * j, 768)]).astype(BF)
        for n in range(3):
            value = out[:, 256 * n : 256 * n + 256]
            if j < 2:
                value = value.astype(F32)
                factor = inverse_norms(value, square)
                if j == 0:
                    row = jnp.zeros((1, 256), F32)
                    for h in range(8):
                        row = jnp.where(lane == h, scale3_ref[8 * n + h], row)
                    factor = factor * row
                value = (value * factor).astype(BF)
            qkv[6 * j + 2 * n] = value[:, :128]
            qkv[6 * j + 2 * n + 1] = value[:, 128:]

    masks = head_masks(4)
    lane = iota((1, 128), 1)
    level = jnp.where(lane < 64, MASK, -MASK).astype(BF)

    def group(g, carry):
        for win in range(2):

            def rows(ref_at):
                return jnp.concatenate(
                    [ref_at(pl.ds(128 * win, 128)), ref_at(pl.ds(256 + 128 * win, 128))], 0
                )

            q, k, v = (rows(lambda r, j=j: qkv[6 * j + g, r, :]) for j in range(3))
            marks = rows(lambda r: aug[r, :])
            keys = jnp.concatenate([k, marks], 1)
            marks = marks * level
            right = jnp.concatenate([v, jnp.ones((256, 128), BF)], 1)
            outs = []
            for h in range(4):
                score = dot_nt(jnp.concatenate([q * masks[h], marks], 1), keys)
                level_h = bias3[4 * g + h, 1]
                spot = jnp.concatenate(
                    [
                        jnp.concatenate([level_h, bias3[4 * g + h, 2]], 1),
                        jnp.concatenate([bias3[4 * g + h, 0], level_h], 1),
                    ],
                    0,
                )
                outs.append(dot(jnp.exp(score + spot).astype(BF), right))
            out = lane_pick([o[:, :128] for o in outs]) / lane_pick([o[:, 128:] for o in outs])
            out = out.astype(BF)
            cols = pl.ds(pl.multiple_of(g * 128, 128), 128)
            ctx[pl.ds(128 * win, 128), cols] = out[:128]
            ctx[pl.ds(256 + 128 * win, 128), cols] = out[128:]
        return carry

    lax.fori_loop(0, 6, group, 0, unroll=2)

    get_up.wait()
    get_down.wait()
    flight_u = both_ways(piece_u, piece_u, 768)
    flight_d = both_ways(piece_d, piece_d, 192)
    late = list(pass_on(piece_a, 768, flight_a) + pass_on(piece_p, 48, flight_p))

    get_proj3.wait()
    y = dot(ctx[...], wproj[...])
    y = layer_norm(y, gain_attn3[...].reshape(1, 768)) + x.astype(F32)
    y = y.astype(BF).astype(F32)
    for half in range(2):
        for r in range(32):
            source = half * 256 + 8 * r
            for m in range(6):
                flat[m, pl.ds(r * 16 + half * 8, 8), :] = y[
                    source : source + 8, 128 * m : 128 * m + 128
                ]
    pieces = []
    for j in range(2):
        side = jnp.concatenate(
            [flat[m, pl.ds(j, 256, stride=2), :] for m in range(6)], 1
        ).reshape(16, 2, 8, 768)
        for i in range(2):
            pieces.append(side[:, i].reshape(128, 768).astype(BF))
    get_merge.wait()
    merged = dot(jnp.concatenate(pieces, 1), wm[...])
    merged = layer_norm(merged, gain_merge[...].reshape(1, 1536)).astype(BF)
    row, col = iota((128, 128), 0), iota((128, 128), 1)
    source = lax.rem(row, 64) // 4 * 8 + row // 64 * 4 + lax.rem(row, 4)
    order = jnp.where(col == source, 1.0, 0.0).astype(BF)
    m4[...] = dot(order, merged).astype(BF).reshape(2, 64, 1536)

    shift = [
        w.go(m4.at[1, pl.ds(0, 48)], back.at[pl.ds(16, 48)], shifted(0, 1)),
        w.go(m4.at[0, pl.ds(48, 16)], back.at[pl.ds(64, 16)], shifted(1, 0)),
        w.go(m4.at[1, pl.ds(48, 16)], back.at[pl.ds(0, 16)], shifted(1, 1)),
    ]
    back[pl.ds(80, 48), :] = m4[0, pl.ds(0, 48), :]
    for c in flight_t:
        c.wait_recv()

    def build4(n, carry):
        s, h = n // 3, lax.rem(n, 3)
        rows = tabs[s, h]
        tables = bias_tables([rows[m : m + 1] for m in range(4)])
        side = jnp.where(core == 0, tables[2], tables[0])
        for a in range(16):
            bias4[n, pl.ds(8 * a, 8), pl.ds(0, 128)] = bias_block(tables[1], a)
            bias4[n, pl.ds(8 * a, 8), pl.ds(128, 128)] = bias_block(side, a)
        return carry

    lax.fori_loop(0, 12, build4, 0)
    for c in shift:
        c.wait_recv()
    source = lax.rem(row, 8) // 4 * 64 + row // 8 * 4 + lax.rem(row, 4)
    order = jnp.where(col == source, 1.0, 0.0).astype(BF)
    blocks[0] = dot(order, back[...]).astype(BF)

    def attend(b):
        both = jnp.concatenate([blocks[b], others[b]], 0)
        qkv4[...] = dot(both, wa[...]).astype(BF)
        outs = []
        for pair in range(2):
            normed = []
            for n in range(3):
                value = qkv4[:, pl.ds(768 * pair + 256 * n, 256)]
                full = value.astype(F32)
                full = full * inverse_norms(full, square)
                for i in range(2):
                    part_of = slice(128 * i, 128 * i + 128)
                    kind = (2 * n + i) % 3
                    normed.append(value[:, part_of] if kind == 2 else full[:, part_of])
            for s in range(2):
                q, k, v = normed[3 * s : 3 * s + 3]
                q = (q[:128] * tabs[2 * pair + s, 0, pl.ds(4, 1), pl.ds(0, 128)]).astype(BF)
                k = k.astype(BF)
                right = jnp.concatenate([v, jnp.ones((256, 128), BF)], 1)
                sums = []
                for h in range(3):
                    score = dot_nt(q * masks[h], k) + bias4[3 * (2 * pair + s) + h]
                    sums.append(dot(jnp.exp(score).astype(BF), right))
                outs.append(
                    (
                        lane_pick([o[:, :128] for o in sums])
                        / lane_pick([o[:, 128:] for o in sums])
                    ).astype(BF)
                )
        part[b] = dot(jnp.concatenate(outs, 1), wp[...].reshape(512, 1536)).astype(BF)

    def feed(b):
        inner = gelu(dot(hidden[b], wu[...])).astype(BF)
        part[b] = dot(inner, wd[...]).astype(BF)

    def ring(held, buf, compute, meet, between):
        right = w.go(held.at[0], held.at[1], along_x(1))
        left = w.go(held.at[0], held.at[2], along_x(-1))
        meet(0)
        compute(0)
        right.wait_recv()
        on_right = w.go(held.at[1, first], held.at[3, first], along_x(1))
        left.wait_recv()
        on_left = w.go(held.at[2, second], held.at[3, second], along_x(-1))
        meet(1)
        compute(1)
        near_left = w.go(part.at[1], buf.at[0], along_x(-1))
        meet(2)
        compute(2)
        near_right = w.go(part.at[2], buf.at[1], along_x(1))
        on_right.wait_recv()
        on_left.wait_recv()
        meet(3)
        compute(3)
        far = w.go(part.at[3], buf.at[2], along_x(2))
        between()
        total = part[0].astype(F32)
        near_left.wait_recv()
        near_right.wait_recv()
        total = total + buf[0].astype(F32) + buf[1].astype(F32)
        far.wait_recv()
        total = total + buf[2].astype(F32)
        for c in (right, left, on_right, on_left, near_left, near_right, far):
            c.wait_send()
        return total

    crossing = []

    def meet_core(b):
        if b == 0:
            crossing.append(w.go(blocks.at[0], others.at[0], other_core()))
            for flight in (flight_a, flight_p):
                flight[2].wait_recv()
            for c in late:
                c.wait_recv()
        if b == 1:
            crossing.append(w.go(blocks.at[1], others.at[1], other_core()))
            crossing.append(w.go(blocks.at[2], others.at[2], other_core()))
        if b == 3:
            crossing.append(w.go(blocks.at[3], others.at[3], other_core()))
        crossing[b].wait_recv()

    later = []

    def pass_mlp():
        later.extend(pass_on(piece_u, 768, flight_u) + pass_on(piece_d, 192, flight_d))

    total = ring(blocks, buf4, attend, meet_core, pass_mlp)
    total = layer_norm(total, gain_attn4[...].reshape(1, 1536))
    hidden[0] = (blocks[0].astype(F32) + total).astype(BF)

    def meet_weights(b):
        if b == 0:
            for flight in (flight_u, flight_d):
                flight[2].wait_recv()
            for c in later:
                c.wait_recv()

    def settle():
        for c in halo + shift + flight_t + crossing + late + later:
            c.wait_send()
        for flight in (flight_a, flight_p, flight_u, flight_d):
            for c in flight:
                c.wait_send()

    total = ring(hidden, bufm, feed, meet_weights, settle)
    total = layer_norm(total, gain_mlp4[...].reshape(1, 1536))
    out_ref[...] = (hidden[0].astype(F32) + total).astype(BF).reshape(16, 8, 1536)


def per_device(
    tokens,
    regions,
    w_qkv3,
    w_proj3,
    bias_table3,
    logit_scale3,
    gain_attn3,
    w_merge,
    gain_merge,
    w_qkv4,
    w_proj4,
    bias_table4,
    logit_scale4,
    gain_attn4,
    w_up4,
    w_down4,
    gain_mlp4,
):
    small = jnp.concatenate(
        [
            jnp.pad(bias_table3, ((0, 0), (0, 1), (0, 97))),
            jnp.pad(bias_table4, ((0, 0), (0, 1), (0, 97))),
            jnp.pad(regions.astype(F32)[None], ((0, 0), (0, 0), (0, 112))),
        ],
        0,
    )
    any_ = pl.BlockSpec(memory_space=pl.ANY)
    vm = pl.BlockSpec(memory_space=pltpu.VMEM)
    sm = pl.BlockSpec(memory_space=pltpu.SMEM)
    out = pl.pallas_call(
        whole_kernel,
        name="whole",
        out_shape=jax.ShapeDtypeStruct((16, 8, 1536), BF),
        in_specs=[any_, vm, sm, sm, any_, any_, vm, any_, vm, any_, any_, vm, any_, any_, vm],
        out_specs=vm,
        scratch_shapes=[
            pltpu.VMEM((512, 768), BF),
            pltpu.VMEM((2, 256, 768), BF),
            pltpu.VMEM((2, 256, 768), BF),
            pltpu.VMEM((512, 128), BF),
            pltpu.VMEM((768, 2304), BF),
            pltpu.VMEM((768, 768), BF),
            pltpu.VMEM((3072, 1536), BF),
            pltpu.VMEM((18, 512, 128), BF),
            pltpu.VMEM((24, 3, 128, 128), F32),
            pltpu.VMEM((6, 512, 128), F32),
            pltpu.VMEM((2, 64, 1536), BF),
            pltpu.VMEM((128, 1536), BF),
            pltpu.VMEM((4, 3, 8, 256), F32),
            pltpu.VMEM((12, 128, 256), F32),
            pltpu.VMEM((3, 1536, 96), BF),
            pltpu.VMEM((1536, 1536), BF),
            pltpu.VMEM((4, 128, 1536), BF),
            pltpu.VMEM((4, 128, 1536), BF),
            pltpu.VMEM((4, 128, 1536), BF),
            pltpu.VMEM((256, 1536), BF),
            pltpu.VMEM((4, 128, 1536), BF),
            pltpu.VMEM((3, 128, 1536), BF),
            pltpu.VMEM((3, 128, 1536), BF),
            pltpu.VMEM((4, 128, 1536), BF),
            pltpu.VMEM((1536, 1536), BF),
            pltpu.VMEM((1536, 1536), BF),
            pltpu.SemaphoreType.DMA((WIRES,)),
            pltpu.SemaphoreType.DMA((WIRES,)),
            pltpu.SemaphoreType.DMA((8,)),
        ],
        compiler_params=pltpu.CompilerParams(
            collective_id=1, has_side_effects=True, vmem_limit_bytes=VMEM_LIMIT
        ),
    )(
        tokens.reshape(512, 768),
        small,
        logit_scale3,
        logit_scale4,
        w_qkv3,
        w_proj3,
        gain_attn3,
        w_merge,
        gain_merge,
        w_qkv4,
        w_proj4,
        gain_attn4,
        w_up4,
        w_down4,
        gain_mlp4,
    )
    return out

def solution(mesh):
    placed = (
        P("wide", "narrow", None),
        P("wide", "narrow"),
        P(),
        P(),
        P(),
        P(),
        P(),
        P(),
        P(),
        P(None, None, "narrow"),
        P("narrow", None),
        P("narrow", None, None),
        P("narrow"),
        P(),
        P(None, "narrow"),
        P("narrow", None),
        P(),
    )
    return jax.shard_map(
        per_device, mesh=mesh, in_specs=placed, out_specs=P("wide", "narrow", None), check_vma=False
    )
```

time: 560 us -> 141 us (0.25)
  waiting for transfers between devices: 269 us -> 0 us
  local copies, waits for them, and re-layouts: 142 us -> 5.08 us
  Pallas kernels: 0 us -> 132 us
  matrix products: 91.1 us -> 0 us
  other arithmetic: 27.1 us -> 1.64 us
  between operations: 13.8 us -> 0.02 us
  starting transfers between devices: 12.6 us -> 0 us
    psum x1 -> x0, waiting for transfers between devices: 154 us -> none  [per_device(): lax.psum(partial_value.astype(jnp.bfloat16), 'narrow').astype(jnp.float32)]
    pallas_call x0 -> x1, Pallas kernels: none -> 132 us  [per_device(): pl.pallas_call(whole_kernel, name='whole', out_shape=jax.ShapeDtypeStruct...]
    add x4 -> x0, local copies, waits for them, and re-layouts: 99.5 us -> none  [attend(): score = score * scale[None, :, None, None] + bias[None]]
    dot_general x14 -> x0, matrix products: 91.1 us -> none  [the longest x2 24.3 us: attend(): jnp.einsum('nqhd,nkhd->nhqk', query, keys, precision=lax.Precision.HIGHEST)]
    unnamed x4 -> x0, waiting for transfers between devices: 76.7 us -> none
    all_gather x1 -> x0, waiting for transfers between devices: 23.5 us -> none  [per_device(): band_tokens = lax.all_gather(merged, 'narrow', axis=1, tiled=True)]
    ppermute x4 -> x0, waiting for transfers between devices: 14.6 us -> none  [from_behind(): return lax.ppermute(block, axis, route)]
    ppermute x4 -> x0, starting transfers between devices: 12.6 us -> none  [from_behind(): return lax.ppermute(block, axis, route)]
  transfers between devices with their start and end apart: 7 -> 0, of which waited for: 6 -> 0; matrix products, arithmetic and copies ran while one was open for 23% -> 0% of each run, Pallas kernels for 0% -> 0%
where the time goes in v2:
time: 141 us; the launch traced here: 139 us
  Pallas kernels  132 us (94%)
  local copies, waits for them, and re-layouts  5.08 us (4%)
  other arithmetic  1.64 us (1%)
    pallas_call x1, Pallas kernels, per_device(): pl.pallas_call(whole_kernel, name='whole', out_shape=jax.ShapeDtypeStruct...  132 us
    unnamed x6, local copies, waits for them, and re-layouts  5.08 us

profile of v2, /device:TPU:1, one launch (start us, length us, event | category | flops | bytes accessed | tf_op | source)
XLA Modules:
  0.0 139.2 jit_solution(4321468958877708247)
XLA Ops:
  0.0 0.0 copy-start
  0.0 0.8 copy.19
  0.9 1.1 copy.18
  1.9 1.6 %select_maximum_fusion.small_ref = f32[28,32,128]{2,1,0:T(8,128)} fusion(f32[1,32,16]{2,1,0:T(8,128)S(1)} %convert_bitcast_fusion, f32[3,31,31]{2,1,0:T(8,128)} %param.28, f32[24,31,31]{2,1,0:T(8,128)S(1)} %copy.18), kind=kLoop, calls=%fused_computation.2 | loop fusion | flops 1146880 | bytes 564588 | tf_op jit(solution)/shard_map/concatenate | solution.py:574
  3.6 0.0 copy-done
  3.6 1.4 %copy.20.wqkv4_hbm = bf16[3,1536,96]{2,1,0:T(8,128)(2,1)} copy(bf16[3,1536,96]{1,2,0:T(8,128)(2,1)S(1)} %copy-done) | data formatting | bytes 1769472 | tf_op args[9]
  5.0 132.4 %whole.1 = bf16[16,8,1536]{2,1,0:T(8,128)(2,1)} custom-call(bf16[512,768]{1,0:T(8,128)(2,1)} %bitcast.3, f32[28,32,128]{2,1,0:T(8,128)} %select_maximum_fusion.small_ref, f32[24]{0:T(128)} %scale3_ref.1, f32[3]{0:T(128)} %scale4_ref.1, bf16[768,2304]{1,0:T(8,128)(2,1)} %wqkv3_hbm.1, bf16[768,768]{1,0:T(8,128)(2,1)} %wproj3_hbm.1, f32[768]{0:T(1024)} %gain_attn3.1, ...), custom_call_target="tpu_custom_call" | custom-call | tf_op jit(solution)/shard_map/whole/pallas_call | solution.py:585
  137.4 1.8 %copy.22 = bf16[16,8,1536]{2,1,0:T(8,128)(2,1)} copy(bf16[16,8,1536]{2,1,0:T(8,128)(2,1)} %whole.1) | data formatting | bytes 786432
  (1 shorter events, 0.0 us)
Async XLA Ops:
  0.0 3.6 %copy-start = (bf16[3,1536,96]{1,2,0:T(8,128)(2,1)S(1)}, bf16[3,1536,96]{1,2,0:T(8,128)(2,1)}, u32[]{:S(2)}) copy-start(bf16[3,1536,96]{1,2,0:T(8,128)(2,1)} %param.26) | copy-start | bytes 2654212

commit v3 on v2

--- a/solution.py
+++ b/solution.py
@@ -10,8 +10,8 @@
 BF = jnp.bfloat16
 F32 = jnp.float32
 MASK = 100.0
-WIRES = 64
-VMEM_LIMIT = 60 << 20
+WIRES = 128
+VMEM_LIMIT = 61 << 20
 
 
 def place():
@@ -37,6 +37,11 @@
         (y // 2) * 4 + lax.rem(wide, 4),
         (narrow // 4) * 4 + lax.rem(y, 2) * 2 + lax.rem(narrow, 2),
     )
+
+
+def along_z(step):
+    wide, narrow = place()
+    return ((wide // 4) * 4 + lax.rem(wide + step + 4, 4), narrow)
 
 
 def other_core():
@@ -186,21 +191,14 @@
     wm,
     qkv,
     bias3,
-    flat,
-    m4,
-    back,
     tabs,
-    bias4,
     wtmp,
     wa,
     wp,
     blocks,
     others,
-    qkv4,
-    part,
     buf4,
-    bufm,
-    hidden,
+    visit,
     wu,
     wd,
     send,
@@ -210,6 +208,13 @@
     w = Wires(send, recv)
     core = lax.rem(lax.axis_index("narrow"), 2)
     first, second = pl.ds(0, 64), pl.ds(64, 64)
+    part = [wqkv.at[pl.ds(128 * b, 128), pl.ds(0, 1536)] for b in range(4)]
+    qkv4 = wqkv.at[pl.ds(512, 256), pl.ds(0, 1536)]
+    visit_part = part[0]
+    back, hidden, bufm = visit, others.at[0], buf4.at[0]
+
+    def bias_rows(n, t, start=0, size=128):
+        return pl.ds(pl.multiple_of((3 * n + t) * 128 + start, 8), size)
 
     loads = []
     for i, (src, dst) in enumerate(
@@ -231,7 +236,7 @@
 
     partners = [shifted(i, j) for i, j in ((0, 1), (1, 0), (1, 1), (0, -1), (-1, 0), (-1, -1))]
     partners += [quad(1, 0), quad(0, 1), quad(1, 1), along_x(1), along_x(-1), along_x(2)]
-    partners += [along_y(1), along_y(-1)]
+    partners += [along_y(1), along_y(-1), along_z(1), along_z(-1)]
     greet(partners, len(partners))
 
     get_tokens.wait()
@@ -279,14 +284,47 @@
     def piece_p(s, rows):
         return wp.at[s, rows]
 
-    def piece_u(s, rows):
-        return wu.at[rows, column(s)]
-
-    def piece_d(s, rows):
-        return wd.at[pl.ds(384 * s + rows.start, rows.size)]
-
-    flight_a = both_ways(piece_a, piece_a, 768)
-    flight_p = both_ways(piece_p, piece_p, 48)
+    plane = lax.rem(lax.axis_index("wide"), 4)
+
+    def eighths(slot, start, count):
+        down = pl.multiple_of(48 * start, 48)
+        if slot is None:
+            return (
+                wup_hbm.at[pl.ds(pl.multiple_of(192 * start, 192), 192 * count)],
+                wdown_hbm.at[pl.ds(down, 48 * count)],
+            )
+        return (
+            wu.at[pl.ds(pl.multiple_of(192 * start, 192), 192 * count), column(slot)],
+            wd.at[pl.ds(384 * slot + down, 48 * count)],
+        )
+
+    def send_mlp(source, target, start, count, device):
+        return [
+            w.go(a, b, device)
+            for a, b in zip(eighths(source, start, count), eighths(target, start, count))
+        ]
+
+    def arrive(copies):
+        for c in copies:
+            c.wait_recv()
+
+    def quarter(step):
+        return 2 * lax.rem(plane + step + 4, 4)
+
+    def spread_z(slot):
+        return (
+            send_mlp(slot, slot, quarter(0), 2, along_z(1)),
+            send_mlp(slot, slot, quarter(0), 2, along_z(-1)),
+        )
+
+    def forward_z(slot, flight):
+        arrive(flight[0])
+        a = send_mlp(slot, slot, quarter(-1), 1, along_z(1))
+        arrive(flight[1])
+        b = send_mlp(slot, slot, quarter(1) + 1, 1, along_z(-1))
+        c = send_mlp(slot, slot + 1, quarter(-1), 2, other_core())
+        c += send_mlp(slot, slot + 1, quarter(1), 2, other_core())
+        return a + b, c
 
     moved = table_rows(small_ref[pl.ds(24, 3)].reshape(96, 128))
     lane = iota((1, 256), 1)
@@ -319,7 +357,7 @@
             tables = bias_tables([row[:, 256 * m : 256 * m + 256] for m in range(4)])
             for t in range(3):
                 for a in range(16):
-                    bias3[4 * g + h, t, pl.ds(8 * a, 8), :] = bias_block(tables[t], a)
+                    bias3[bias_rows(4 * g + h, t, 8 * a, 8), :] = bias_block(tables[t], a)
         return carry
 
     lax.fori_loop(0, 6, build3, 0)
@@ -327,6 +365,9 @@
     get_qkv3.wait()
     for c in halo:
         c.wait_recv()
+    flight_a = both_ways(piece_a, piece_a, 768)
+    flight_p = both_ways(piece_p, piece_p, 48)
+    across = send_mlp(None, 4, quarter(0), 2, along_x(2))
     x = xr[...].reshape(512, 768)
     square = head_blocks()
     lane = iota((1, 256), 1) // HD
@@ -366,11 +407,11 @@
             outs = []
             for h in range(4):
                 score = dot_nt(jnp.concatenate([q * masks[h], marks], 1), keys)
-                level_h = bias3[4 * g + h, 1]
+                side = [bias3[bias_rows(4 * g + h, t), :] for t in range(3)]
                 spot = jnp.concatenate(
                     [
-                        jnp.concatenate([level_h, bias3[4 * g + h, 2]], 1),
-                        jnp.concatenate([bias3[4 * g + h, 0], level_h], 1),
+                        jnp.concatenate([side[1], side[2]], 1),
+                        jnp.concatenate([side[0], side[1]], 1),
                     ],
                     0,
                 )
@@ -384,12 +425,6 @@
 
     lax.fori_loop(0, 6, group, 0, unroll=2)
 
-    get_up.wait()
-    get_down.wait()
-    flight_u = both_ways(piece_u, piece_u, 768)
-    flight_d = both_ways(piece_d, piece_d, 192)
-    late = list(pass_on(piece_a, 768, flight_a) + pass_on(piece_p, 48, flight_p))
-
     get_proj3.wait()
     y = dot(ctx[...], wproj[...])
     y = layer_norm(y, gain_attn3[...].reshape(1, 768)) + x.astype(F32)
@@ -398,13 +433,13 @@
         for r in range(32):
             source = half * 256 + 8 * r
             for m in range(6):
-                flat[m, pl.ds(r * 16 + half * 8, 8), :] = y[
+                bias3[pl.ds(512 * m + r * 16 + half * 8, 8), :] = y[
                     source : source + 8, 128 * m : 128 * m + 128
                 ]
     pieces = []
     for j in range(2):
         side = jnp.concatenate(
-            [flat[m, pl.ds(j, 256, stride=2), :] for m in range(6)], 1
+            [bias3[pl.ds(512 * m + j, 256, stride=2), :] for m in range(6)], 1
         ).reshape(16, 2, 8, 768)
         for i in range(2):
             pieces.append(side[:, i].reshape(128, 768).astype(BF))
@@ -414,14 +449,15 @@
     row, col = iota((128, 128), 0), iota((128, 128), 1)
     source = lax.rem(row, 64) // 4 * 8 + row // 64 * 4 + lax.rem(row, 4)
     order = jnp.where(col == source, 1.0, 0.0).astype(BF)
-    m4[...] = dot(order, merged).astype(BF).reshape(2, 64, 1536)
+    m4 = part[0]
+    m4[...] = dot(order, merged).astype(BF)
 
     shift = [
-        w.go(m4.at[1, pl.ds(0, 48)], back.at[pl.ds(16, 48)], shifted(0, 1)),
-        w.go(m4.at[0, pl.ds(48, 16)], back.at[pl.ds(64, 16)], shifted(1, 0)),
-        w.go(m4.at[1, pl.ds(48, 16)], back.at[pl.ds(0, 16)], shifted(1, 1)),
+        w.go(m4.at[pl.ds(64, 48)], back.at[pl.ds(16, 48)], shifted(0, 1)),
+        w.go(m4.at[pl.ds(48, 16)], back.at[pl.ds(64, 16)], shifted(1, 0)),
+        w.go(m4.at[pl.ds(112, 16)], back.at[pl.ds(0, 16)], shifted(1, 1)),
     ]
-    back[pl.ds(80, 48), :] = m4[0, pl.ds(0, 48), :]
+    back[pl.ds(80, 48), :] = m4[pl.ds(0, 48), :]
     for c in flight_t:
         c.wait_recv()
 
@@ -431,13 +467,25 @@
         tables = bias_tables([rows[m : m + 1] for m in range(4)])
         side = jnp.where(core == 0, tables[2], tables[0])
         for a in range(16):
-            bias4[n, pl.ds(8 * a, 8), pl.ds(0, 128)] = bias_block(tables[1], a)
-            bias4[n, pl.ds(8 * a, 8), pl.ds(128, 128)] = bias_block(side, a)
+            bias3[bias_rows(n, 0, 8 * a, 8), :] = bias_block(tables[1], a)
+            bias3[bias_rows(n, 1, 8 * a, 8), :] = bias_block(side, a)
         return carry
 
     lax.fori_loop(0, 12, build4, 0)
     for c in shift:
-        c.wait_recv()
+        c.wait()
+    late = list(pass_on(piece_a, 768, flight_a) + pass_on(piece_p, 48, flight_p))
+    arrive(across)
+    spread4 = spread_z(4)
+    skew = send_mlp(4, 6, quarter(0), 1, along_y(1))
+    skew += send_mlp(4, 6, quarter(0) + 1, 1, along_y(-1))
+    mates = send_mlp(4, 5, quarter(0), 2, other_core())
+    get_up.wait()
+    get_down.wait()
+    beside = send_mlp(0, 2, 0, 4, along_y(1))
+    beside += send_mlp(0, 2, 4, 4, along_y(-1))
+    mates += send_mlp(0, 1, 0, 8, other_core())
+    onward = []
     source = lax.rem(row, 8) // 4 * 64 + row // 8 * 4 + lax.rem(row, 4)
     order = jnp.where(col == source, 1.0, 0.0).astype(BF)
     blocks[0] = dot(order, back[...]).astype(BF)
@@ -463,7 +511,11 @@
                 right = jnp.concatenate([v, jnp.ones((256, 128), BF)], 1)
                 sums = []
                 for h in range(3):
-                    score = dot_nt(q * masks[h], k) + bias4[3 * (2 * pair + s) + h]
+                    n = 3 * (2 * pair + s) + h
+                    spot = jnp.concatenate(
+                        [bias3[bias_rows(n, 0), :], bias3[bias_rows(n, 1), :]], 1
+                    )
+                    score = dot_nt(q * masks[h], k) + spot
                     sums.append(dot(jnp.exp(score).astype(BF), right))
                 outs.append(
                     (
@@ -471,34 +523,33 @@
                         / lane_pick([o[:, 128:] for o in sums])
                     ).astype(BF)
                 )
-        part[b] = dot(jnp.concatenate(outs, 1), wp[...].reshape(512, 1536)).astype(BF)
-
-    def feed(b):
-        inner = gelu(dot(hidden[b], wu[...])).astype(BF)
-        part[b] = dot(inner, wd[...]).astype(BF)
-
-    def ring(held, buf, compute, meet, between):
+        part[b][...] = dot(jnp.concatenate(outs, 1), wp[...].reshape(512, 1536)).astype(BF)
+
+    def ring(held, buf, compute, meet, after):
         right = w.go(held.at[0], held.at[1], along_x(1))
         left = w.go(held.at[0], held.at[2], along_x(-1))
         meet(0)
         compute(0)
+        after(0)
         right.wait_recv()
         on_right = w.go(held.at[1, first], held.at[3, first], along_x(1))
         left.wait_recv()
         on_left = w.go(held.at[2, second], held.at[3, second], along_x(-1))
         meet(1)
         compute(1)
-        near_left = w.go(part.at[1], buf.at[0], along_x(-1))
+        near_left = w.go(part[1], buf.at[0], along_x(-1))
+        after(1)
         meet(2)
         compute(2)
-        near_right = w.go(part.at[2], buf.at[1], along_x(1))
+        near_right = w.go(part[2], buf.at[1], along_x(1))
+        after(2)
         on_right.wait_recv()
         on_left.wait_recv()
         meet(3)
         compute(3)
-        far = w.go(part.at[3], buf.at[2], along_x(2))
-        between()
-        total = part[0].astype(F32)
+        far = w.go(part[3], buf.at[2], along_x(2))
+        after(3)
+        total = part[0][...].astype(F32)
         near_left.wait_recv()
         near_right.wait_recv()
         total = total + buf[0].astype(F32) + buf[1].astype(F32)
@@ -524,32 +575,65 @@
             crossing.append(w.go(blocks.at[3], others.at[3], other_core()))
         crossing[b].wait_recv()
 
-    later = []
-
-    def pass_mlp():
-        later.extend(pass_on(piece_u, 768, flight_u) + pass_on(piece_d, 192, flight_d))
-
-    total = ring(blocks, buf4, attend, meet_core, pass_mlp)
+    spread6 = []
+    ends = []
+
+    def after(b):
+        if b == 0:
+            arrive(skew)
+            spread6.extend(spread_z(6))
+            mates.extend(send_mlp(6, 7, quarter(0), 2, other_core()))
+        if b == 1:
+            a, c = forward_z(4, spread4)
+            ends.append((4, a))
+            mates.extend(c)
+        if b == 3:
+            a, c = forward_z(6, spread6)
+            ends.append((6, a))
+            mates.extend(c)
+            arrive(beside)
+            mates.extend(send_mlp(2, 3, 0, 8, other_core()))
+
+    total = ring(blocks, buf4, attend, meet_core, after)
     total = layer_norm(total, gain_attn4[...].reshape(1, 1536))
-    hidden[0] = (blocks[0].astype(F32) + total).astype(BF)
-
-    def meet_weights(b):
-        if b == 0:
-            for flight in (flight_u, flight_d):
-                flight[2].wait_recv()
-            for c in later:
-                c.wait_recv()
-
-    def settle():
-        for c in halo + shift + flight_t + crossing + late + later:
-            c.wait_send()
-        for flight in (flight_a, flight_p, flight_u, flight_d):
-            for c in flight:
-                c.wait_send()
-
-    total = ring(hidden, bufm, feed, meet_weights, settle)
-    total = layer_norm(total, gain_mlp4[...].reshape(1, 1536))
-    out_ref[...] = (hidden[0].astype(F32) + total).astype(BF).reshape(16, 8, 1536)
+    hidden[...] = (blocks[0].astype(F32) + total).astype(BF)
+
+    visits = [
+        w.go(hidden.at[first], visit.at[first], along_x(1)),
+        w.go(hidden.at[second], visit.at[second], along_x(-1)),
+    ]
+
+    def units(tokens, half):
+        return gelu(dot(tokens, wu[:, pl.ds(1536 * half, 1536)])).astype(BF)
+
+    for slot, copies in ends:
+        arrive(copies)
+        mates.extend(send_mlp(slot, slot + 1, quarter(2), 2, other_core()))
+    arrive(mates)
+    own = dot(units(hidden[...], 0), wd[pl.ds(0, 1536), :])
+    arrive(visits)
+    guest = dot(units(visit[...], 0), wd[pl.ds(0, 1536), :])
+    inner = units(visit[...], 1)
+    returns = []
+    for n in range(2):
+        cols = pl.ds(768 * n, 768)
+        value = guest[:, 768 * n : 768 * n + 768] + dot(inner, wd[pl.ds(1536, 1536), cols])
+        visit_part[:, cols] = value.astype(BF)
+        returns += [
+            w.go(visit_part.at[first, cols], bufm.at[first, cols], along_x(-1)),
+            w.go(visit_part.at[second, cols], bufm.at[second, cols], along_x(1)),
+        ]
+    own = own + dot(units(hidden[...], 1), wd[pl.ds(1536, 1536), :])
+    sent = halo + flight_t + crossing + late + across + skew + beside + mates
+    for f in spread4 + tuple(spread6) + flight_a + flight_p:
+        sent += f if isinstance(f, list) else [f]
+    for slot, copies in ends:
+        sent += copies
+    for c in sent + visits + returns:
+        c.wait_send()
+    arrive(returns)
+    total = layer_norm(own + bufm[...].astype(F32), gain_mlp4[...].reshape(1, 1536))
+    out_ref[...] = (hidden[...].astype(F32) + total).astype(BF).reshape(16, 8, 1536)
 
 
 def per_device(
@@ -597,24 +681,17 @@
             pltpu.VMEM((768, 768), BF),
             pltpu.VMEM((3072, 1536), BF),
             pltpu.VMEM((18, 512, 128), BF),
-            pltpu.VMEM((24, 3, 128, 128), F32),
-            pltpu.VMEM((6, 512, 128), F32),
-            pltpu.VMEM((2, 64, 1536), BF),
-            pltpu.VMEM((128, 1536), BF),
+            pltpu.VMEM((72 * 128, 128), F32),
             pltpu.VMEM((4, 3, 8, 256), F32),
-            pltpu.VMEM((12, 128, 256), F32),
             pltpu.VMEM((3, 1536, 96), BF),
             pltpu.VMEM((1536, 1536), BF),
             pltpu.VMEM((4, 128, 1536), BF),
             pltpu.VMEM((4, 128, 1536), BF),
             pltpu.VMEM((4, 128, 1536), BF),
-            pltpu.VMEM((256, 1536), BF),
-            pltpu.VMEM((4, 128, 1536), BF),
             pltpu.VMEM((3, 128, 1536), BF),
-            pltpu.VMEM((3, 128, 1536), BF),
-            pltpu.VMEM((4, 128, 1536), BF),
-            pltpu.VMEM((1536, 1536), BF),
-            pltpu.VMEM((1536, 1536), BF),
+            pltpu.VMEM((128, 1536), BF),
+            pltpu.VMEM((1536, 3072), BF),
+            pltpu.VMEM((3072, 1536), BF),
             pltpu.SemaphoreType.DMA((WIRES,)),
             pltpu.SemaphoreType.DMA((WIRES,)),
             pltpu.SemaphoreType.DMA((8,)),

time: 141 us -> 106 us (0.75)
  Pallas kernels: 132 us -> 98.3 us
    pallas_call x1, Pallas kernels: 132 us -> 98.3 us  [per_device(): pl.pallas_call(whole_kernel, name='whole', out_shape=jax.ShapeDtypeStruct...]
where the time goes in v3:
time: 106 us; the launch traced here: 105 us
  Pallas kernels  98.3 us (93%)
  local copies, waits for them, and re-layouts  5.08 us (5%)
  other arithmetic  1.64 us (2%)
    pallas_call x1, Pallas kernels, per_device(): pl.pallas_call(whole_kernel, name='whole', out_shape=jax.ShapeDtypeStruct...  98.3 us
    unnamed x6, local copies, waits for them, and re-layouts  5.08 us

profile of v3, /device:TPU:1, one launch (start us, length us, event | category | flops | bytes accessed | tf_op | source)
XLA Modules:
  0.0 105.1 jit_solution(18326843162973597304)
XLA Ops:
  0.0 0.0 copy-start
  0.0 0.8 copy.19
  0.9 1.1 %copy.18 = f32[24,31,31]{2,1,0:T(8,128)S(1)} copy(f32[24,31,31]{2,0,1:T(8,128)} %param.21) | data formatting | bytes 184512 | tf_op args[4]
  1.9 1.6 %select_maximum_fusion.small_ref = f32[28,32,128]{2,1,0:T(8,128)} fusion(f32[1,32,16]{2,1,0:T(8,128)S(1)} %convert_bitcast_fusion, f32[3,31,31]{2,1,0:T(8,128)} %param.28, f32[24,31,31]{2,1,0:T(8,128)S(1)} %copy.18), kind=kLoop, calls=%fused_computation.2 | loop fusion | flops 1146880 | bytes 564588 | tf_op jit(solution)/shard_map/concatenate | solution.py:658
  3.6 0.0 copy-done
  3.6 1.4 %copy.20.wqkv4_hbm = bf16[3,1536,96]{2,1,0:T(8,128)(2,1)} copy(bf16[3,1536,96]{1,2,0:T(8,128)(2,1)S(1)} %copy-done) | data formatting | bytes 1769472 | tf_op args[9]
  5.0 98.3 %whole.1 = bf16[16,8,1536]{2,1,0:T(8,128)(2,1)} custom-call(bf16[512,768]{1,0:T(8,128)(2,1)} %bitcast.3, f32[28,32,128]{2,1,0:T(8,128)} %select_maximum_fusion.small_ref, f32[24]{0:T(128)} %scale3_ref.1, f32[3]{0:T(128)} %scale4_ref.1, bf16[768,2304]{1,0:T(8,128)(2,1)} %wqkv3_hbm.1, bf16[768,768]{1,0:T(8,128)(2,1)} %wproj3_hbm.1, f32[768]{0:T(1024)} %gain_attn3.1, ...), custom_call_target="tpu_custom_call" | custom-call | tf_op jit(solution)/shard_map/whole/pallas_call | solution.py:669
  103.3 1.8 %copy.22 = bf16[16,8,1536]{2,1,0:T(8,128)(2,1)} copy(bf16[16,8,1536]{2,1,0:T(8,128)(2,1)} %whole.1) | data formatting | bytes 786432
  (1 shorter events, 0.0 us)
Async XLA Ops:
  0.0 3.6 %copy-start = (bf16[3,1536,96]{1,2,0:T(8,128)(2,1)S(1)}, bf16[3,1536,96]{1,2,0:T(8,128)(2,1)}, u32[]{:S(2)}) copy-start(bf16[3,1536,96]{1,2,0:T(8,128)(2,1)} %param.26) | copy-start | bytes 2654212

commit v4 on v3

--- a/solution.py
+++ b/solution.py
@@ -132,20 +132,20 @@
     return [jnp.where(lane == h, 1.0, 0.0).astype(BF) for h in range(count)]
 
 
-def table_rows(tables):
-    lane = iota((256, 1024), 1)
-    spot = lax.rem(iota((256, 1024), 0), 128)
-    pick = jnp.where(spot == 31 - 8 * (lane // 256) - lax.rem(lane, 8), 1.0, 0.0).astype(BF)
-    high = tables.astype(BF)
-    low = (tables - high.astype(F32)).astype(BF)
-    moved = dot(jnp.concatenate([high, low], 1), pick)
-    row = lax.rem(iota(moved.shape, 0), 32)
+def table_rows(logits, each):
+    lane = iota((31, 1024), 1)
+    column = 31 - 8 * (lane // 256) - lax.rem(lane, 8)
+    pick = jnp.where(iota((31, 1024), 0) == column, 1.0, 0.0).astype(BF)
+    high = logits.astype(BF)
+    low = (logits - high.astype(F32)).astype(BF)
+    moved = dot(high, pick) + dot(low, pick)
+    row = iota(moved.shape, 0) // each
     f = lax.rem(iota(moved.shape, 1), 256) // 8
-    return jnp.where(row == 30 - f, moved, 0.0)
-
-
-def head_row(moved, head):
-    values = jnp.sum(moved[32 * head : 32 * head + 32], 0, keepdims=True)
+    moved = jnp.where(row == 30 - f, moved, 0.0)
+    if each == 1:
+        values = jnp.sum(moved, 0, keepdims=True)
+    else:
+        values = jnp.sum(moved.reshape(31, each, 1024), 0)
     return 16.0 / (1.0 + jnp.exp(-values))
 
 
@@ -167,7 +167,9 @@
 
 def whole_kernel(
     tokens_ref,
-    small_ref,
+    labels_ref,
+    table3_ref,
+    table4_ref,
     scale3_ref,
     scale4_ref,
     wqkv3_hbm,
@@ -252,9 +254,8 @@
 
     get_qkv4.wait()
     for j in range(3):
-        wa[:, pl.ds(128 * j, 128)] = jnp.concatenate(
-            [wtmp[j].astype(F32), jnp.zeros((1536, 32), F32)], 1
-        ).astype(BF)
+        wide = jnp.concatenate([wtmp[j].astype(F32), jnp.zeros((32, 1536), F32)], 0)
+        wa[:, pl.ds(128 * j, 128)] = wide.T.astype(BF)
     get_proj4.wait()
     for s in range(4):
         wp[s, pl.ds(96, 32), :] = jnp.zeros((32, 1536), BF)
@@ -326,10 +327,9 @@
         c += send_mlp(slot, slot + 1, quarter(1), 2, other_core())
         return a + b, c
 
-    moved = table_rows(small_ref[pl.ds(24, 3)].reshape(96, 128))
     lane = iota((1, 256), 1)
     for h in range(3):
-        row = head_row(moved, h)
+        row = table_rows(table4_ref[h], 1)
         for m in range(4):
             tabs[0, h, pl.ds(m, 1), :] = row[:, 256 * m : 256 * m + 256]
     tabs[0, 0, pl.ds(4, 1), :] = jnp.where(
@@ -341,32 +341,34 @@
         w.go(tabs.at[0], tabs.at[3], quad(1, 1)),
     ]
 
-    token = iota((512, 32), 0)
-    rows = jnp.where(lax.rem(token, 256) // 8 == iota((512, 32), 1), 1.0, 0.0).astype(BF)
-    labels = dot(rows, small_ref[27].astype(BF))
-    token = iota((512, 128), 0)
+    token = iota((512, 16), 0)
+    pick = token // 256 * 8 + lax.rem(token, 8) == iota((512, 16), 1)
+    labels = dot(jnp.where(pick, 1.0, 0.0).astype(BF), labels_ref[...].astype(F32).astype(BF))
+    pick = lax.rem(iota((512, 32), 0), 256) // 8 == iota((512, 32), 1)
+    labels = jnp.where(pick, labels, 0.0).astype(BF)
     at = iota((512, 128), 1)
-    labels = jnp.where(at == token // 256 * 8 + lax.rem(token, 8), labels, 0.0).astype(BF)
-    labels = dot(labels, jnp.ones((128, 128), BF))
+    labels = dot(labels, jnp.ones((32, 128), BF))
     aug[...] = jnp.where((labels == at.astype(F32)) | (at == 64), 1.0, 0.0).astype(BF)
 
-    def build3(g, carry):
-        moved = table_rows(small_ref[pl.ds(4 * g, 4)].reshape(128, 128))
-        for h in range(4):
-            row = head_row(moved, h)
-            tables = bias_tables([row[:, 256 * m : 256 * m + 256] for m in range(4)])
+
+    def build3(i, carry):
+        heads = pl.ds(pl.multiple_of(8 * i, 8), 8)
+        values = table_rows(table3_ref[:, heads, :].reshape(248, 31), 8)
+        for h in range(8):
+            tables = bias_tables([values[h : h + 1, 256 * m : 256 * m + 256] for m in range(4)])
             for t in range(3):
                 for a in range(16):
-                    bias3[bias_rows(4 * g + h, t, 8 * a, 8), :] = bias_block(tables[t], a)
+                    bias3[bias_rows(8 * i + h, t, 8 * a, 8), :] = bias_block(tables[t], a)
         return carry
 
-    lax.fori_loop(0, 6, build3, 0)
+    lax.fori_loop(0, 3, build3, 0)
+
+    flight_a = both_ways(piece_a, piece_a, 768)
+    flight_p = both_ways(piece_p, piece_p, 48)
 
     get_qkv3.wait()
     for c in halo:
         c.wait_recv()
-    flight_a = both_ways(piece_a, piece_a, 768)
-    flight_p = both_ways(piece_p, piece_p, 48)
     across = send_mlp(None, 4, quarter(0), 2, along_x(2))
     x = xr[...].reshape(512, 768)
     square = head_blocks()
@@ -484,7 +486,7 @@
     get_down.wait()
     beside = send_mlp(0, 2, 0, 4, along_y(1))
     beside += send_mlp(0, 2, 4, 4, along_y(-1))
-    mates += send_mlp(0, 1, 0, 8, other_core())
+    mates_low = send_mlp(0, 1, 0, 8, other_core())
     onward = []
     source = lax.rem(row, 8) // 4 * 64 + row // 8 * 4 + lax.rem(row, 4)
     order = jnp.where(col == source, 1.0, 0.0).astype(BF)
@@ -592,7 +594,7 @@
             ends.append((6, a))
             mates.extend(c)
             arrive(beside)
-            mates.extend(send_mlp(2, 3, 0, 8, other_core()))
+            mates_low.extend(send_mlp(2, 3, 0, 8, other_core()))
 
     total = ring(blocks, buf4, attend, meet_core, after)
     total = layer_norm(total, gain_attn4[...].reshape(1, 1536))
@@ -606,13 +608,14 @@
     def units(tokens, half):
         return gelu(dot(tokens, wu[:, pl.ds(1536 * half, 1536)])).astype(BF)
 
+    arrive(mates_low)
+    own = dot(units(hidden[...], 0), wd[pl.ds(0, 1536), :])
     for slot, copies in ends:
         arrive(copies)
         mates.extend(send_mlp(slot, slot + 1, quarter(2), 2, other_core()))
-    arrive(mates)
-    own = dot(units(hidden[...], 0), wd[pl.ds(0, 1536), :])
     arrive(visits)
     guest = dot(units(visit[...], 0), wd[pl.ds(0, 1536), :])
+    arrive(mates)
     inner = units(visit[...], 1)
     returns = []
     for n in range(2):
@@ -624,7 +627,7 @@
             w.go(visit_part.at[second, cols], bufm.at[second, cols], along_x(1)),
         ]
     own = own + dot(units(hidden[...], 1), wd[pl.ds(1536, 1536), :])
-    sent = halo + flight_t + crossing + late + across + skew + beside + mates
+    sent = halo + flight_t + crossing + late + across + skew + beside + mates + mates_low
     for f in spread4 + tuple(spread6) + flight_a + flight_p:
         sent += f if isinstance(f, list) else [f]
     for slot, copies in ends:
@@ -655,14 +658,6 @@
     w_down4,
     gain_mlp4,
 ):
-    small = jnp.concatenate(
-        [
-            jnp.pad(bias_table3, ((0, 0), (0, 1), (0, 97))),
-            jnp.pad(bias_table4, ((0, 0), (0, 1), (0, 97))),
-            jnp.pad(regions.astype(F32)[None], ((0, 0), (0, 0), (0, 112))),
-        ],
-        0,
-    )
     any_ = pl.BlockSpec(memory_space=pl.ANY)
     vm = pl.BlockSpec(memory_space=pltpu.VMEM)
     sm = pl.BlockSpec(memory_space=pltpu.SMEM)
@@ -670,7 +665,7 @@
         whole_kernel,
         name="whole",
         out_shape=jax.ShapeDtypeStruct((16, 8, 1536), BF),
-        in_specs=[any_, vm, sm, sm, any_, any_, vm, any_, vm, any_, any_, vm, any_, any_, vm],
+        in_specs=[any_, vm, vm, vm, sm, sm, any_, any_, vm, any_, vm, any_, any_, vm, any_, any_, vm],
         out_specs=vm,
         scratch_shapes=[
             pltpu.VMEM((512, 768), BF),
@@ -683,7 +678,7 @@
             pltpu.VMEM((18, 512, 128), BF),
             pltpu.VMEM((72 * 128, 128), F32),
             pltpu.VMEM((4, 3, 8, 256), F32),
-            pltpu.VMEM((3, 1536, 96), BF),
+            pltpu.VMEM((3, 96, 1536), BF),
             pltpu.VMEM((1536, 1536), BF),
             pltpu.VMEM((4, 128, 1536), BF),
             pltpu.VMEM((4, 128, 1536), BF),
@@ -701,7 +696,9 @@
         ),
     )(
         tokens.reshape(512, 768),
-        small,
+        regions.T,
+        bias_table3.transpose(1, 0, 2),
+        bias_table4,
         logit_scale3,
         logit_scale4,
         w_qkv3,
@@ -709,7 +706,7 @@
         gain_attn3,
         w_merge,
         gain_merge,
-        w_qkv4,
+        w_qkv4.transpose(0, 2, 1),
         w_proj4,
         gain_attn4,
         w_up4,

time: 106 us -> 94.8 us (0.89)
  Pallas kernels: 98.3 us -> 91.8 us
  local copies, waits for them, and re-layouts: 5.08 us -> 1.77 us
  other arithmetic: 1.64 us -> 0 us
    pallas_call x1, Pallas kernels: 98.3 us -> 91.8 us  [per_device(): pl.pallas_call(whole_kernel, name='whole', out_shape=jax.ShapeDtypeStruct...]
    unnamed x6 -> x1, local copies, waits for them, and re-layouts: 5.08 us -> 1.77 us
    concatenate x1 -> x0, other arithmetic: 1.63 us -> none  [per_device(): jnp.concatenate([jnp.pad(bias_table3, ((0, 0), (0, 1), (0, 97))), jnp.pad...]
where the time goes in v4:
time: 94.8 us; the launch traced here: 93.6 us
  Pallas kernels  91.8 us (97%)
  local copies, waits for them, and re-layouts  1.77 us (2%)
    pallas_call x1, Pallas kernels, per_device(): pl.pallas_call(whole_kernel, name='whole', out_shape=jax.ShapeDtypeStruct...  91.8 us

profile of v4, /device:TPU:1, one launch (start us, length us, event | category | flops | bytes accessed | tf_op | source)
XLA Modules:
  0.0 93.6 jit_solution(9730703396747831195)
XLA Ops:
  0.0 91.8 %whole.1 = bf16[16,8,1536]{2,1,0:T(8,128)(2,1)} custom-call(bf16[512,768]{1,0:T(8,128)(2,1)} %bitcast.5, s32[16,32]{1,0:T(8,128)} %bitcast.7, f32[31,24,31]{2,1,0:T(8,128)} %bitcast.6, f32[3,31,31]{2,1,0:T(8,128)} %table4_ref.1, f32[24]{0:T(128)} %scale3_ref.1, f32[3]{0:T(128)} %scale4_ref.1, bf16[768,2304]{1,0:T(8,128)(2,1)} %wqkv3_hbm.1, ...), custom_call_target="tpu_custom_call" | custom-call | tf_op jit(solution)/shard_map/whole/pallas_call | solution.py:664
  91.9 1.8 %copy.19 = bf16[16,8,1536]{2,1,0:T(8,128)(2,1)} copy(bf16[16,8,1536]{2,1,0:T(8,128)(2,1)} %whole.1) | data formatting | bytes 786432

commit v5 on v4

--- a/solution.py
+++ b/solution.py
@@ -213,7 +213,7 @@
     part = [wqkv.at[pl.ds(128 * b, 128), pl.ds(0, 1536)] for b in range(4)]
     qkv4 = wqkv.at[pl.ds(512, 256), pl.ds(0, 1536)]
     visit_part = part[0]
-    back, hidden, bufm = visit, others.at[0], buf4.at[0]
+    back, hidden, bufm = visit, others.at[0], buf4.at[2]
 
     def bias_rows(n, t, start=0, size=128):
         return pl.ds(pl.multiple_of((3 * n + t) * 128 + start, 8), size)
@@ -476,6 +476,13 @@
     lax.fori_loop(0, 12, build4, 0)
     for c in shift:
         c.wait()
+    source = lax.rem(row, 8) // 4 * 64 + row // 8 * 4 + lax.rem(row, 4)
+    order = jnp.where(col == source, 1.0, 0.0).astype(BF)
+    blocks[0] = dot(order, back[...]).astype(BF)
+    right = w.go(blocks.at[0], blocks.at[1], along_x(1))
+    left = w.go(blocks.at[0], blocks.at[2], along_x(-1))
+    crossing = [w.go(blocks.at[0], others.at[0], other_core())]
+
     late = list(pass_on(piece_a, 768, flight_a) + pass_on(piece_p, 48, flight_p))
     arrive(across)
     spread4 = spread_z(4)
@@ -484,13 +491,8 @@
     mates = send_mlp(4, 5, quarter(0), 2, other_core())
     get_up.wait()
     get_down.wait()
-    beside = send_mlp(0, 2, 0, 4, along_y(1))
-    beside += send_mlp(0, 2, 4, 4, along_y(-1))
     mates_low = send_mlp(0, 1, 0, 8, other_core())
-    onward = []
-    source = lax.rem(row, 8) // 4 * 64 + row // 8 * 4 + lax.rem(row, 4)
-    order = jnp.where(col == source, 1.0, 0.0).astype(BF)
-    blocks[0] = dot(order, back[...]).astype(BF)
+    beside, spread6, ends = [], [], []
 
     def attend(b):
         both = jnp.concatenate([blocks[b], others[b]], 0)
@@ -527,76 +529,55 @@
                 )
         part[b][...] = dot(jnp.concatenate(outs, 1), wp[...].reshape(512, 1536)).astype(BF)
 
-    def ring(held, buf, compute, meet, after):
-        right = w.go(held.at[0], held.at[1], along_x(1))
-        left = w.go(held.at[0], held.at[2], along_x(-1))
-        meet(0)
-        compute(0)
-        after(0)
-        right.wait_recv()
-        on_right = w.go(held.at[1, first], held.at[3, first], along_x(1))
-        left.wait_recv()
-        on_left = w.go(held.at[2, second], held.at[3, second], along_x(-1))
-        meet(1)
-        compute(1)
-        near_left = w.go(part[1], buf.at[0], along_x(-1))
-        after(1)
-        meet(2)
-        compute(2)
-        near_right = w.go(part[2], buf.at[1], along_x(1))
-        after(2)
-        on_right.wait_recv()
-        on_left.wait_recv()
-        meet(3)
-        compute(3)
-        far = w.go(part[3], buf.at[2], along_x(2))
-        after(3)
-        total = part[0][...].astype(F32)
-        near_left.wait_recv()
-        near_right.wait_recv()
-        total = total + buf[0].astype(F32) + buf[1].astype(F32)
-        far.wait_recv()
-        total = total + buf[2].astype(F32)
-        for c in (right, left, on_right, on_left, near_left, near_right, far):
-            c.wait_send()
-        return total
-
-    crossing = []
-
-    def meet_core(b):
-        if b == 0:
-            crossing.append(w.go(blocks.at[0], others.at[0], other_core()))
-            for flight in (flight_a, flight_p):
-                flight[2].wait_recv()
-            for c in late:
-                c.wait_recv()
-        if b == 1:
-            crossing.append(w.go(blocks.at[1], others.at[1], other_core()))
-            crossing.append(w.go(blocks.at[2], others.at[2], other_core()))
-        if b == 3:
-            crossing.append(w.go(blocks.at[3], others.at[3], other_core()))
-        crossing[b].wait_recv()
-
-    spread6 = []
-    ends = []
-
-    def after(b):
-        if b == 0:
-            arrive(skew)
-            spread6.extend(spread_z(6))
-            mates.extend(send_mlp(6, 7, quarter(0), 2, other_core()))
-        if b == 1:
-            a, c = forward_z(4, spread4)
-            ends.append((4, a))
-            mates.extend(c)
-        if b == 3:
-            a, c = forward_z(6, spread6)
-            ends.append((6, a))
-            mates.extend(c)
-            arrive(beside)
-            mates_low.extend(send_mlp(2, 3, 0, 8, other_core()))
-
-    total = ring(blocks, buf4, attend, meet_core, after)
+    for flight in (flight_a, flight_p):
+        flight[2].wait_recv()
+    arrive(late)
+    crossing[0].wait_recv()
+    attend(0)
+    beside += send_mlp(0, 2, 0, 4, along_y(1))
+    beside += send_mlp(0, 2, 4, 4, along_y(-1))
+    right.wait_recv()
+    crossing.append(w.go(blocks.at[1], others.at[1], other_core()))
+    on_right = w.go(blocks.at[1, first], blocks.at[3, first], along_x(1))
+    left.wait_recv()
+    crossing.append(w.go(blocks.at[2], others.at[2], other_core()))
+    on_left = w.go(blocks.at[2, second], blocks.at[3, second], along_x(-1))
+    crossing[1].wait_recv()
+    attend(1)
+    sums = [w.go(part[1].at[first], buf4.at[1, first], along_x(-1))]
+    arrive(skew)
+    spread6 += spread_z(6)
+    mates += send_mlp(6, 7, quarter(0), 2, other_core())
+    crossing[2].wait_recv()
+    attend(2)
+    sums.append(w.go(part[2].at[second], buf4.at[0, second], along_x(1)))
+    on_right.wait_recv()
+    crossing.append(w.go(blocks.at[3, first], others.at[3, first], other_core()))
+    on_left.wait_recv()
+    crossing.append(w.go(blocks.at[3, second], others.at[3, second], other_core()))
+    crossing[3].wait_recv()
+    crossing[4].wait_recv()
+    attend(3)
+    far_right = w.go(part[3].at[first], buf4.at[2, first], along_x(1))
+    far_left = w.go(part[3].at[second], buf4.at[2, second], along_x(-1))
+    far_right.wait_recv()
+    part[2][first, :] = (part[2][first, :].astype(F32) + buf4[2, first, :].astype(F32)).astype(BF)
+    sums.append(w.go(part[2].at[first], buf4.at[0, first], along_x(1)))
+    far_left.wait_recv()
+    part[1][second, :] = (
+        part[1][second, :].astype(F32) + buf4[2, second, :].astype(F32)
+    ).astype(BF)
+    sums.append(w.go(part[1].at[second], buf4.at[1, second], along_x(-1)))
+    for slot, flight in ((4, spread4), (6, spread6)):
+        onward, copies = forward_z(slot, flight)
+        ends.append((slot, onward))
+        mates += copies
+    arrive(beside)
+    mates_low += send_mlp(2, 3, 0, 8, other_core())
+    arrive(sums)
+    total = part[0][...].astype(F32) + buf4[0].astype(F32) + buf4[1].astype(F32)
+    for c in [right, left, on_right, on_left, far_right, far_left] + sums:
+        c.wait_send()
     total = layer_norm(total, gain_attn4[...].reshape(1, 1536))
     hidden[...] = (blocks[0].astype(F32) + total).astype(BF)
 

time: 94.8 us -> 93.2 us (0.983)
  Pallas kernels: 91.8 us -> 89.8 us
    pallas_call x1, Pallas kernels: 91.8 us -> 89.8 us  [per_device(): pl.pallas_call(whole_kernel, name='whole', out_shape=jax.ShapeDtypeStruct...]
where the time goes in v5:
time: 93.2 us; the launch traced here: 91.6 us
  Pallas kernels  89.8 us (96%)
  local copies, waits for them, and re-layouts  1.77 us (2%)
    pallas_call x1, Pallas kernels, per_device(): pl.pallas_call(whole_kernel, name='whole', out_shape=jax.ShapeDtypeStruct...  89.8 us

profile of v5, /device:TPU:1, one launch (start us, length us, event | category | flops | bytes accessed | tf_op | source)
XLA Modules:
  0.0 91.6 jit_solution(16938534235932063120)
XLA Ops:
  0.0 89.8 %whole.1 = bf16[16,8,1536]{2,1,0:T(8,128)(2,1)} custom-call(bf16[512,768]{1,0:T(8,128)(2,1)} %bitcast.5, s32[16,32]{1,0:T(8,128)} %bitcast.7, f32[31,24,31]{2,1,0:T(8,128)} %bitcast.6, f32[3,31,31]{2,1,0:T(8,128)} %table4_ref.1, f32[24]{0:T(128)} %scale3_ref.1, f32[3]{0:T(128)} %scale4_ref.1, bf16[768,2304]{1,0:T(8,128)(2,1)} %wqkv3_hbm.1, ...), custom_call_target="tpu_custom_call" | custom-call | tf_op jit(solution)/shard_map/whole/pallas_call | solution.py:645
  89.8 1.8 %copy.19 = bf16[16,8,1536]{2,1,0:T(8,128)(2,1)} copy(bf16[16,8,1536]{2,1,0:T(8,128)(2,1)} %whole.1) | data formatting | bytes 786432

commit v6 on v5

--- a/solution.py
+++ b/solution.py
@@ -162,7 +162,11 @@
 
 
 def bias_block(table, a):
-    return pltpu.roll(table, (256 - 8 * (15 - a)) % 256, 1)[:, :128]
+    far = 8 * (15 - a)
+    if far == 0:
+        return table[:, :128]
+    mixed = jnp.where(iota((8, 128), 1) >= far, table[:, :128], table[:, 128:])
+    return pltpu.roll(mixed, 128 - far, 1)
 
 
 def whole_kernel(

time: 93.2 us -> 101 us (1.084)
  the two profiles are of different devices: /device:TPU:1 before, /device:TPU:33 now
where the time goes in v6:
time: 101 us
  Pallas kernels  99.1 us (98%)
  local copies, waits for them, and re-layouts  1.77 us (2%)
    pallas_call x1, Pallas kernels, per_device(): pl.pallas_call(whole_kernel, name='whole', out_shape=jax.ShapeDtypeStruct...  99.1 us

profile of v6, /device:TPU:33, one launch (start us, length us, event | category | flops | bytes accessed | tf_op | source)
XLA Modules:
  0.0 100.9 jit_solution(2246127201283637503)
XLA Ops:
  0.0 99.1 %whole.1 = bf16[16,8,1536]{2,1,0:T(8,128)(2,1)} custom-call(bf16[512,768]{1,0:T(8,128)(2,1)} %bitcast.5, s32[16,32]{1,0:T(8,128)} %bitcast.7, f32[31,24,31]{2,1,0:T(8,128)} %bitcast.6, f32[3,31,31]{2,1,0:T(8,128)} %table4_ref.1, f32[24]{0:T(128)} %scale3_ref.1, f32[3]{0:T(128)} %scale4_ref.1, bf16[768,2304]{1,0:T(8,128)(2,1)} %wqkv3_hbm.1, ...), custom_call_target="tpu_custom_call" | custom-call | tf_op jit(solution)/shard_map/whole/pallas_call | solution.py:649
  99.1 1.8 %copy.19 = bf16[16,8,1536]{2,1,0:T(8,128)(2,1)} copy(bf16[16,8,1536]{2,1,0:T(8,128)(2,1)} %whole.1) | data formatting | bytes 786432
